TPU v7x, 256 devices: a whole 4x4x8 slice. The times are simulated.
256 devices in a mesh: dp: 4 (over x), owner: 64 (over y, z, core).
Axes of the slice: x: 4, y: 4, z: 8, core: 2. Of those that a mesh axis runs over, the one named last changes fastest.
Arguments:
- vectors: bfloat16 [196608, 1024], P(('dp', 'owner')), may hold values from -6 to 6
- meso_labels: int32 [196608], P(('dp', 'owner')), may hold values from 0 to 2047, as said below
- fine_labels: int32 [196608], P(('dp', 'owner')), may hold values from 0 to 63
- meso_centroids: float32 [2048, 1024], P('owner'), may hold values from -6 to 6
- fine_centroids: bfloat16 [2048, 64, 1024], P('owner'), may hold values from -4 to 4
Outputs:
- nearest: float32 [196608], P(('dp', 'owner'))
- new_meso: float32 [2048, 1024], P('owner')
- new_fine: float32 [2048, 64, 1024], P('owner', 'dp')
Inputs may be any that keep to these rules, and one draw needn't show every extreme that they name: `meso_labels`: each vector's mesocluster lies in the block of 32 owned by one index of owner; among the vectors of one device, those whose mesocluster belongs to one owner and whose fine label lies in one aligned block of 16 number at most 6, and this many in every draw.
All inputs are finite; a program needn't handle non-finite values.
Results may differ from a plain program's by a relative error of at most 0.0003.
Values may be sent and summed in bfloat16 or wider, within the bound.
A program may use at most 64 MiB of HBM per device.

v0:
```python
import jax
import jax.numpy as jnp
from jax import lax
from jax.sharding import PartitionSpec as P

smoothing = 1.0


def nearest_of(members, code_words, fine_centroids, fine_count):
    feat_width = members.shape[-1]
    flat_rows = members.reshape(-1, feat_width)
    flat_codes = code_words.reshape(-1)
    centroid_table = fine_centroids.reshape(-1, feat_width)
    column_meso = jnp.arange(centroid_table.shape[0], dtype=jnp.int32) // fine_count
    cross_terms = lax.dot_general(
        flat_rows, centroid_table, (((1,), (1,)), ((), ())), preferred_element_type=jnp.float32
    )
    row_norms = jnp.einsum("rd,rd->r", flat_rows, flat_rows, preferred_element_type=jnp.float32)
    cent_norms = jnp.einsum(
        "kd,kd->k", centroid_table, centroid_table, preferred_element_type=jnp.float32
    )
    distance = row_norms[:, None] - 2.0 * cross_terms + cent_norms[None, :]
    same_meso = column_meso[None, :] == (flat_codes // fine_count)[:, None]
    closest = jnp.min(jnp.where(same_meso, distance, jnp.inf), axis=1) / feat_width
    closest = jnp.where(flat_codes >= 0, closest, 0.0)
    return closest.reshape(code_words.shape)


def member_sums(members, column_ids, column_total):
    feat_width = members.shape[-1]
    flat_rows = members.reshape(-1, feat_width)
    flat_ids = column_ids.reshape(-1)
    one_hot = (flat_ids[:, None] == jnp.arange(column_total, dtype=jnp.int32)[None, :]).astype(
        jnp.bfloat16
    )
    column_sums = lax.dot_general(
        one_hot, flat_rows, (((0,), (0,)), ((), ())), preferred_element_type=jnp.float32
    )
    column_counts = jnp.sum(one_hot, axis=0, dtype=jnp.float32)
    return (column_sums, column_counts)


def body(vectors, meso_labels, fine_labels, meso_centroids, fine_centroids):
    owner_total = lax.axis_size("owner")
    dp_total = lax.axis_size("dp")
    row_count, feat_width = vectors.shape
    meso_dev = meso_centroids.shape[0]
    fine_count = fine_centroids.shape[1]
    group_size = fine_count // dp_total
    bin_total = owner_total * dp_total
    slot_count = 2 * row_count // bin_total
    owner_of = meso_labels // meso_dev
    group_of = fine_labels // group_size
    bin_of = owner_of * dp_total + group_of
    bin_hits = (bin_of[:, None] == jnp.arange(bin_total, dtype=jnp.int32)[None, :]).astype(
        jnp.int32
    )
    bin_rank = jnp.sum((jnp.cumsum(bin_hits, axis=0) - bin_hits) * bin_hits, axis=1)
    slot_index = bin_of * slot_count + bin_rank
    code_word = meso_labels % meso_dev * fine_count + fine_labels
    packed = (
        jnp.zeros((bin_total * slot_count, feat_width), jnp.bfloat16).at[slot_index].set(vectors)
    )
    packed = packed.reshape(owner_total, dp_total, slot_count, feat_width)
    packed_codes = jnp.full((bin_total * slot_count,), -1, jnp.int32).at[slot_index].set(code_word)
    packed_codes = packed_codes.reshape(owner_total, dp_total, slot_count)
    my_group = lax.axis_index("dp")
    members, member_codes = (
        lax.all_to_all(packed, "owner", split_axis=0, concat_axis=0, tiled=True),
        lax.all_to_all(packed_codes, "owner", split_axis=0, concat_axis=0, tiled=True),
    )
    closest = nearest_of(members, member_codes, fine_centroids, fine_count)
    all_sums, all_counts = member_sums(members, member_codes, meso_dev * fine_count)
    group_sums, group_counts = (
        lax.psum_scatter(
            all_sums.reshape(meso_dev, fine_count, feat_width),
            "dp",
            scatter_dimension=1,
            tiled=True,
        ),
        lax.psum_scatter(
            all_counts.reshape(meso_dev, fine_count), "dp", scatter_dimension=1, tiled=True
        ),
    )
    returned = lax.all_to_all(closest, "owner", split_axis=0, concat_axis=0, tiled=True)
    nearest = returned.reshape(-1)[slot_index]
    meso_part = jnp.sum(group_sums, axis=1)
    meso_cnt = jnp.sum(group_counts, axis=1)
    share_width = feat_width // dp_total
    tiled_counts = jnp.broadcast_to(meso_cnt[:, None], (meso_dev, dp_total))
    part_sums, part_counts = (
        lax.psum_scatter(meso_part, "dp", scatter_dimension=1, tiled=True),
        lax.psum_scatter(tiled_counts, "dp", scatter_dimension=1, tiled=True),
    )
    old_share = lax.dynamic_slice_in_dim(meso_centroids, my_group * share_width, share_width, 1)
    new_share = (part_sums + smoothing * old_share) / (part_counts + smoothing)
    new_meso = lax.all_gather(new_share, "dp", axis=1, tiled=True)
    meso_shift = new_meso - meso_centroids
    own_fine = lax.dynamic_slice_in_dim(
        fine_centroids, my_group * group_size, group_size, 1
    ).astype(jnp.float32)
    new_fine = (group_sums + smoothing * (own_fine + meso_shift[:, None, :])) / (
        group_counts[:, :, None] + smoothing
    )
    return (nearest, new_meso, new_fine)


def solution(mesh):
    return jax.shard_map(
        body,
        mesh=mesh,
        in_specs=(
            P(("dp", "owner"), None),
            P(("dp", "owner")),
            P(("dp", "owner")),
            P("owner", None),
            P("owner", None, None),
        ),
        out_specs=(P(("dp", "owner")), P("owner", None), P("owner", "dp", None)),
        check_vma=False,
    )
```

profile of v0, /device:TPU:8, one launch (start us, length us, event | category | flops | bytes accessed | tf_op | source)
XLA Modules:
  0.0 279.9 jit_solution(768848082320849153)
XLA Ops:
  7.2 0.7 fusion.23
  7.9 0.1 copy.14
  8.0 0.2 fusion.9
  8.2 0.1 broadcast_add_fusion
  8.3 0.3 copy.15
  8.6 0.3 fusion.12
  8.9 3.4 %scatter_custom_fusion = s32[1536]{0:T(1024)S(1)} fusion(s32[768]{0:T(1024)S(1)} %compare_select_fusion.1, s32[768]{0:T(1024)S(1)} %get-tuple-element.3, s32[]{:T(128)} %constant.80.clone.1), kind=kCustom, calls=%fused_computation.65 | custom fusion | bytes 6148 | tf_op jit(solution)/shard_map/scatter | solution.py:65
  12.3 0.9 reshape.116
  13.1 12.1 %all-to-all-start = ((s32[64,4,6]{2,1,0:T(4,128)}), s32[64,4,6]{2,1,0:T(4,128)S(1)}, u32[]{:S(2)}, u32[]{:S(2)}) async-start(s32[64,4,6]{2,1,0:T(4,128)} %reshape.116), calls=%async_computation | async-start | bytes 262144 | tf_op jit(solution)/shard_map/all_to_all | solution.py:70
  25.3 7.6 %scatter_custom_fusion.1 = bf16[1536,1024]{1,0:T(8,128)(2,1)S(1)} fusion(s32[768]{0:T(1024)S(1)} %compare_select_fusion.1, bf16[768,1024]{1,0:T(8,128)(2,1)} %param.5, bf16[]{:T(256)} %constant.92.clone.1), kind=kCustom, calls=%fused_computation.16 | custom fusion | bytes 3146240 | tf_op jit(solution)/shard_map/scatter | solution.py:62
  32.9 2.9 %reshape.118 = bf16[64,4,6,1024]{3,2,1,0:T(8,128)(2,1)} reshape(bf16[1536,1024]{1,0:T(8,128)(2,1)S(1)} %scatter_custom_fusion.1) | data formatting | bytes 6291456 | tf_op jit(solution)/shard_map/reshape | solution.py:64
  35.8 10.1 %copy.16 = bf16[64,4,6,1024]{3,1,2,0:T(4,128)(2,1)} copy(bf16[64,4,6,1024]{3,2,1,0:T(8,128)(2,1)} %reshape.118) | data formatting | bytes 6291456 | tf_op jit(solution)/shard_map/reshape | solution.py:64
  45.9 0.0 all-to-all-done
  45.9 10.3 %all-to-all-start.1 = ((bf16[64,4,6,1024]{3,1,2,0:T(4,128)(2,1)}), bf16[64,4,6,1024]{3,1,2,0:T(4,128)(2,1)S(1)}, u32[]{:S(2)}, u32[]{:S(2)}) async-start(bf16[64,4,6,1024]{3,1,2,0:T(4,128)(2,1)} %copy.16), calls=%async_computation.1 | async-start | bytes 6291456 | tf_op jit(solution)/shard_map/all_to_all | solution.py:69
  56.2 0.0 reduce-scatter.10.cloned.1.call-start
  56.3 0.2 reshape.117
  56.5 1.4 convert_reduce_fusion
  57.9 0.1 reshape.122
  57.9 0.7 copy.26
  58.6 0.0 reduce-scatter.10.cloned.1.call-update
  58.7 0.3 reduce-scatter.6.cloned.1.call-start
  58.9 69.7 %all-to-all-done.1 = bf16[64,4,6,1024]{3,1,2,0:T(4,128)(2,1)S(1)} async-done(((bf16[64,4,6,1024]{3,1,2,0:T(4,128)(2,1)}), bf16[64,4,6,1024]{3,1,2,0:T(4,128)(2,1)S(1)}, u32[]{:S(2)}, u32[]{:S(2)}) %all-to-all-start.1) | async-done | bytes 3145760 | tf_op jit(solution)/shard_map/all_to_all | solution.py:69
  128.6 3.6 %copy.17 = bf16[64,4,6,1024]{3,2,1,0:T(8,128)(2,1)} copy(bf16[64,4,6,1024]{3,1,2,0:T(4,128)(2,1)S(1)} %all-to-all-done.1) | data formatting | bytes 6291456 | tf_op jit(solution)/shard_map/all_to_all | solution.py:69
  132.2 4.9 %reshape.154 = bf16[1536,1024,1]{1,0,2:T(8,128)(2,1)S(1)} reshape(bf16[64,4,6,1024]{3,2,1,0:T(8,128)(2,1)} %copy.17) | data formatting | bytes 6291456 | tf_op jit(solution)/shard_map/reshape | solution.py:11
  137.1 8.9 %fusion.1 = f32[32,64,1024]{2,1,0:T(8,128)} fusion(bf16[1536,1024,1]{1,0,2:T(8,128)(2,1)S(1)} %reshape.154, s32[32,64]{1,0:T(8,128)S(1)} %multiply_add_fusion, s32[1536]{0:T(1024)S(1)} %reshape.117), kind=kOutput, calls=%fused_computation.7 | convolution fusion | flops 6445596672 | bytes 11548672 | tf_op jit(solution)/shard_map/dot_general | solution.py:36
  146.0 0.0 copy-start.2
  146.0 0.0 reduce-scatter.6.cloned.1.call-update
  146.0 0.0 reduce-scatter.8.cloned.1.call-start
  146.0 0.6 copy-done.2
  146.6 0.6 dynamic-slice
  147.2 3.1 %fusion.3 = f32[2048]{0:T(1024)S(1)} fusion(bf16[32,64,1024]{2,1,0:T(8,128)(2,1)} %param.9), kind=kLoop, calls=%fused_computation.10 | loop fusion | flops 6289408 | bytes 4202496 | tf_op jit(solution)/shard_map/kd,kd->k/dot_general | solution.py:19
  150.3 0.0 reduce-scatter.10.cloned.1.call-done
  150.4 0.8 copy.27
  151.1 0.7 bitcast_reduce_fusion
  151.9 10.5 %all-reduce = f32[32,4]{0,1:T(4,128)S(1)} all-reduce(f32[32,4]{0,1:T(4,128)S(1)} %broadcast_in_dim.21), channel_id=5, replica_groups=mesh['dp'=4,'owner'=64] {'dp'}, use_global_device_ids=true, to_apply=%region_12.13.clone | all-reduce | flops 128 | bytes 1024
  162.4 4.9 %reshape.119 = bf16[1536,1024]{1,0:T(8,128)(2,1)S(1)} reshape(bf16[64,4,6,1024]{3,2,1,0:T(8,128)(2,1)} %copy.17) | data formatting | bytes 6291456 | tf_op jit(solution)/shard_map/reshape | solution.py:11
  167.3 0.7 fusion.4
  168.0 10.7 %select_reduce_fusion = f32[1536]{0:T(1024)S(1)} fusion(bf16[1536,1024]{1,0:T(8,128)(2,1)S(1)} %reshape.119, bf16[2048,1024]{1,0:T(8,128)(2,1)} %bitcast.23, f32[2048]{0:T(1024)S(1)} %fusion.3, f32[1536]{0:T(1024)S(1)} %fusion.4, s32[2048]{0:T(1024)S(1)} %add_select_fusion.1, s32[1536]{0:T(1024)S(1)} %add_select_fusion), kind=kOutput, calls=%fused_computation.5 | convolution fusion | flops 6461323776 | bytes 7374848 | tf_op jit(solution)/shard_map/dot_general | solution.py:15
  178.7 0.2 div.81
  178.9 0.0 copy-start.1
  178.9 48.3 %reduce-scatter.6.cloned.1.call-done = f32[32,16,1024]{2,1,0:T(8,128)} async-done(((f32[32,64,1024]{2,1,0:T(8,128)}), f32[32,16,1024]{2,1,0:T(8,128)}) %reduce-scatter.6.cloned.1.call-update) | async-done | bytes 2097168 | tf_op jit(solution)/shard_map/reduce_scatter | solution.py:75
  227.3 2.6 reduce_sum.37
  229.9 0.0 copy-start
  229.9 0.0 reduce-scatter.8.cloned.1.call-update
  229.9 0.7 compare_select_fusion
  230.6 10.5 %all-to-all-start.2 = ((f32[64,4,6]{2,1,0:T(4,128)}), f32[64,4,6]{2,1,0:T(4,128)S(1)}, u32[]{:S(2)}, u32[]{:S(2)}) async-start(f32[64,4,6]{2,1,0:T(4,128)} %compare_select_fusion), calls=%async_computation.2 | async-start | bytes 262144 | tf_op jit(solution)/shard_map/all_to_all | solution.py:85
  241.1 0.7 fusion.29
  241.8 8.7 %all-to-all-done.2 = f32[64,4,6]{2,1,0:T(4,128)S(1)} async-done(((f32[64,4,6]{2,1,0:T(4,128)}), f32[64,4,6]{2,1,0:T(4,128)S(1)}, u32[]{:S(2)}, u32[]{:S(2)}) %all-to-all-start.2) | async-done | bytes 6176 | tf_op jit(solution)/shard_map/all_to_all | solution.py:85
  250.5 0.2 reshape.121
  250.7 6.1 %gather_fusion = f32[768]{0:T(1024)} fusion(f32[1536]{0:T(1024)S(1)} %reshape.121, s32[1024]{0:T(1024)S(1)} %pad_clamp_fusion), kind=kCustom, calls=%fused_computation | custom fusion | bytes 9216 | tf_op jit(solution)/shard_map/gather | solution.py:86
  256.8 0.0 reduce-scatter.8.cloned.1.call-done
  256.8 0.0 copy-done.1
  256.8 0.8 add_divide_fusion.1
  257.7 12.0 %all_gather.3 = f32[32,1024]{1,0:T(8,128)S(1)} all-gather(f32[32,256]{1,0:T(8,128)S(1)} %add_divide_fusion.1), channel_id=1, replica_groups=mesh['dp'=4,'owner'=64] {'dp'}, dimensions={1}, use_global_device_ids=true | all-gather | bytes 163840 | tf_op jit(solution)/shard_map/all_gather | solution.py:97
  269.7 0.0 copy-done
  269.7 3.0 %add_divide_fusion = f32[32,16,1024]{2,1,0:T(8,128)} fusion(f32[32,16,1024]{2,1,0:T(8,128)S(1)} %copy-done, f32[32,16]{1,0:T(8,128)S(1)} %broadcast_add_fusion.1, f32[32,1024]{1,0:T(8,128)S(1)} %sub.43, bf16[32,64,1024]{2,1,0:T(8,128)(2,1)} %param.9, s32[]{:T(128)S(6)} %select_n.62), kind=kLoop, calls=%fused_computation.15 | loop fusion | flops 2097152 | bytes 5376004 | tf_op jit(solution)/shard_map/div | solution.py:102
  272.7 0.7 copy.30
  (11 shorter events, 0.1 us)
Async XLA Ops:
  13.1 32.7 %all-to-all-start = ((s32[64,4,6]{2,1,0:T(4,128)}), s32[64,4,6]{2,1,0:T(4,128)S(1)}, u32[]{:S(2)}, u32[]{:S(2)}) async-start(s32[64,4,6]{2,1,0:T(4,128)} %reshape.116), calls=%async_computation | async-start | bytes 262144 | tf_op jit(solution)/shard_map/all_to_all | solution.py:70
  45.9 82.7 %all-to-all-start.1 = ((bf16[64,4,6,1024]{3,1,2,0:T(4,128)(2,1)}), bf16[64,4,6,1024]{3,1,2,0:T(4,128)(2,1)S(1)}, u32[]{:S(2)}, u32[]{:S(2)}) async-start(bf16[64,4,6,1024]{3,1,2,0:T(4,128)(2,1)} %copy.16), calls=%async_computation.1 | async-start | bytes 6291456 | tf_op jit(solution)/shard_map/all_to_all | solution.py:69
  56.2 94.1 %reduce-scatter.10.cloned.1.call-start = ((), (), s32[]{:S(2)}) async-start(), calls=%async_computation.8 | async-start | bytes 40960
  58.7 168.6 %reduce-scatter.6.cloned.1.call-start = ((), (), s32[]{:S(2)}) async-start(), calls=%async_computation.6 | async-start | bytes 10485760 | tf_op jit(solution)/shard_map/reduce_scatter | solution.py:75
  146.0 0.7 copy-start.2
  146.0 110.8 %reduce-scatter.8.cloned.1.call-start = ((), (), s32[]{:S(2)}) async-start(), calls=%async_computation.7 | async-start | bytes 163840 | tf_op jit(solution)/shard_map/reduce_scatter | solution.py:92
  178.9 77.9 %copy-start.1 = (f32[32,1024]{1,0:T(8,128)S(1)}, f32[32,1024]{1,0:T(8,128)}, u32[]{:S(2)}) copy-start(f32[32,1024]{1,0:T(8,128)} %param.8) | copy-start | bytes 393220
  229.9 39.8 %copy-start = (f32[32,16,1024]{2,1,0:T(8,128)S(1)}, f32[32,16,1024]{2,1,0:T(8,128)}, u32[]{:S(2)}) copy-start(f32[32,16,1024]{2,1,0:T(8,128)} %reduce-scatter.6.cloned.1.call-done) | copy-start | bytes 6291460
  230.6 19.9 %all-to-all-start.2 = ((f32[64,4,6]{2,1,0:T(4,128)}), f32[64,4,6]{2,1,0:T(4,128)S(1)}, u32[]{:S(2)}, u32[]{:S(2)}) async-start(f32[64,4,6]{2,1,0:T(4,128)} %compare_select_fusion), calls=%async_computation.2 | async-start | bytes 262144 | tf_op jit(solution)/shard_map/all_to_all | solution.py:85
Sparse Core Ops, SparseCore 0:
  60.1 23.8 reduce-scatter.9
  146.1 81.1 reduce-scatter.5
  230.5 22.5 reduce-scatter.7
where the time goes:
time: 281 us; the launch traced here: 280 us
  waiting for transfers between devices  127 us (45%)
  local copies, waits for them, and re-layouts  48.7 us (17%)
  starting transfers between devices  33.2 us (12%)
  blocking collectives  22.5 us (8%)
  matrix products  19.6 us (7%)
  other arithmetic  15.1 us (5%)
  between operations  14 us (5%)
    all_to_all x1, waiting for transfers between devices, body(): lax.all_to_all(packed, 'owner', split_axis=0, concat_axis=0, tiled=True)  69.7 us
    reduce_scatter x1, waiting for transfers between devices, body(): lax.psum_scatter(all_sums.reshape(meso_dev, fine_count, feat_width), 'dp'...  48.3 us
    reshape x2, local copies, waits for them, and re-layouts, body(): packed = packed.reshape(owner_total, dp_total, slot_count, feat_width)  13 us
    all_to_all x1, starting transfers between devices, body(): lax.all_to_all(packed_codes, 'owner', split_axis=0, concat_axis=0, tiled=...  12.1 us
    all_gather x1, blocking collectives, body(): new_meso = lax.all_gather(new_share, 'dp', axis=1, tiled=True)  12 us
    dot_general x1, matrix products, nearest_of(): lax.dot_general(flat_rows, centroid_table, (((1,), (1,)), ((), ())), pref...  10.7 us
    unnamed x1, blocking collectives  10.5 us
    all_to_all x1, starting transfers between devices, body(): lax.all_to_all(closest, 'owner', split_axis=0, concat_axis=0, tiled=True)  10.5 us
  transfers between devices with their start and end apart: 6, of which 3 were waited for; matrix products, arithmetic and copies ran while one was open for 25% of the time, Pallas kernels for 0%

commit v1 on v0

v1 whole, which is shorter than its diff:
```python
import functools

import jax
import jax.numpy as jnp
from jax import lax
from jax.experimental import pallas as pl
from jax.experimental.pallas import tpu as pltpu
from jax.sharding import PartitionSpec as P

MESH = pl.DeviceIdType.MESH
D = 1024
ROWS = 768
KF = 64
MESO_DEV = 32
FGROUP = 16
SLOTS = 6
NX, NY, NZ, NC = 4, 4, 8, 2
CHUNKS = NY
WAYS = 8
BLOCK = WAYS * SLOTS
CHUNK_ROWS = WAYS * BLOCK
BINS = CHUNKS * WAYS * WAYS
LANES = 128
KIND = ("zx", "zx", "zx", "xz")
ORDER = (0, 3, 1, 2)

F32, BF16, I32 = jnp.float32, jnp.bfloat16, jnp.int32
NT = (((1,), (1,)), ((), ()))
TN = (((0,), (0,)), ((), ()))


def iota(shape, dim):
    return lax.broadcasted_iota(I32, shape, dim)


def div6(v):
    return (v * 10923) >> 16


def div48(v):
    return div6(v >> 3)


def split3(v):
    first = v.astype(BF16)
    rest = v - first.astype(F32)
    second = rest.astype(BF16)
    third = (rest - second.astype(F32)).astype(BF16)
    return (first, second, third)


def dot(a, b, dims=(((1,), (0,)), ((), ()))):
    return lax.dot_general(a, b, dims, preferred_element_type=F32)


def kernel(
    meso_ref, fine_ref, vec_hbm, old_hbm, cent_hbm,
    near_ref, new_meso_ref, new_fine_ref,
    vec, old, cent, half_norm, perm, packed, got1, mid, got2,
    code1, code1_got, code2, ret1, ret1_got, ret2,
    sums, counts, msum, mcount, part, part_got,
    load_sem, s1_send, s1_recv, s2_send, s2_recv, c1_send, c1_recv, c2_send, c2_recv,
    r1_send, r1_recv, r2_send, r2_recv, p_send, p_recv,
):
    x = lax.axis_index("dp")
    own = lax.axis_index("owner")
    y, z, c = own // 16, lax.rem(own // 2, 8), lax.rem(own, 2)

    def yz_peer(dy, dz):
        return (x, (lax.rem(y + dy, NY) * NZ + lax.rem(z + dz, NZ)) * NC + c)

    def xc_peer(j):
        return (lax.rem(x + j // NC, NX), (y * NZ + z) * NC + lax.rem(c + j % NC, NC))

    def peer(q, hop, way):
        over_z = (KIND[q] == "zx") == (hop == 1)
        if over_z:
            return None if q == 0 and way == 0 else yz_peer(q, way)
        return None if way == 0 else xc_peer(way)

    def peer_back(q, hop, way):
        over_z = (KIND[q] == "zx") == (hop == 1)
        if over_z:
            return None if q == 0 and way == 0 else yz_peer((NY - q) % NY, (NZ - way) % NZ)
        return None if way == 0 else xc_peer(((NX - way // NC) % NX) * NC + way % NC)

    sent = []

    def send(src, dst, send_sem, recv_sem, device):
        copy = pltpu.make_async_remote_copy(
            src_ref=src, dst_ref=dst, send_sem=send_sem, recv_sem=recv_sem,
            device_id=device, device_id_type=MESH,
        )
        copy.start()
        sent.append(copy)

    def arrived(dst, send_sem, recv_sem):
        pltpu.make_async_remote_copy(
            src_ref=dst, dst_ref=dst, send_sem=send_sem, recv_sem=recv_sem,
            device_id=(x, own), device_id_type=MESH,
        ).wait_recv()

    load_vec = pltpu.make_async_copy(vec_hbm, vec, load_sem.at[0])
    load_cent = pltpu.make_async_copy(cent_hbm, cent, load_sem.at[1])
    load_old = pltpu.make_async_copy(old_hbm, old, load_sem.at[2])
    load_vec.start()
    load_cent.start()
    load_old.start()

    barrier = pltpu.get_barrier_semaphore()
    partners = 0
    for dy in range(NY):
        for dz in range(NZ):
            if dy or dz:
                pl.semaphore_signal(barrier, 1, device_id=yz_peer(dy, dz), device_id_type=MESH)
                partners += 1
    for j in range(1, WAYS):
        pl.semaphore_signal(barrier, 1, device_id=xc_peer(j), device_id_type=MESH)
        partners += 1

    meso = meso_ref[...]
    fine = fine_ref[...]
    to = meso >> 5
    dy = ((to >> 4) - y) & 3
    dz = (((to >> 1) & 7) - z) & 7
    way = ((((fine >> 4) - x) & 3) << 1) + ((to - c) & 1)
    x_first = functools.reduce(jnp.logical_or, [dy == q for q in range(CHUNKS) if KIND[q] == "xz"])
    hop1 = jnp.where(x_first, way, dz)
    hop2 = jnp.where(x_first, dz, way)
    first = (dy << 3) + hop1
    bin_of = (first << 3) + hop2
    in_bin = iota((BINS, ROWS), 0) == bin_of
    bin_hot = in_bin.astype(F32).astype(BF16)
    before = (iota((ROWS, ROWS), 0) < iota((ROWS, ROWS), 1)).astype(F32).astype(BF16)
    rank = jnp.sum(jnp.where(in_bin, dot(bin_hot, before), 0.0), axis=0, keepdims=True).astype(I32)
    slot = bin_of * SLOTS + rank

    first_hit = iota((CHUNKS * WAYS, ROWS), 0) == first
    lane_hot = (iota((LANES, ROWS), 0) == hop2 * SLOTS + rank).astype(F32).astype(BF16)
    meso_rows = jnp.where(first_hit, ((meso & 31) + 1).astype(F32), 0.0).astype(BF16)
    fine_rows = jnp.where(first_hit, (fine & 15).astype(F32), 0.0).astype(BF16)
    codes = 16.0 * dot(meso_rows, lane_hot, NT) + dot(fine_rows, lane_hot, NT) - 16.0
    for r in range(CHUNKS * WAYS):
        code1[r] = codes[r : r + 1, :]

    out_row = iota((CHUNK_ROWS, CHUNK_ROWS), 0)
    in_row = iota((CHUNK_ROWS, CHUNK_ROWS), 1)
    out_pair, in_pair = div6(out_row), div6(in_row)
    swapped = ((out_pair & 7) << 3) + (out_pair >> 3)
    perm[...] = (in_row - 6 * in_pair + 6 * swapped == out_row - 6 * out_pair + 6 * in_pair).astype(F32).astype(BF16)

    def pack(q):
        hot = (iota((CHUNK_ROWS, ROWS), 0) + q * CHUNK_ROWS == slot).astype(F32).astype(BF16)
        packed[q] = dot(hot, vec[...]).astype(BF16)

    def hop1_rows(q):
        for way in range(WAYS):
            at = q * WAYS + way
            rows = pl.ds(way * BLOCK, BLOCK)
            to = peer(q, 1, way)
            if to is None:
                got1[q, rows, :] = packed[q, rows, :]
            else:
                send(packed.at[q, rows], got1.at[q, rows], s1_send.at[at], s1_recv.at[at], to)

    load_vec.wait()
    pack(ORDER[0])
    pl.semaphore_wait(barrier, partners)
    for n, q in enumerate(ORDER):
        if n:
            pack(q)
        for way in range(WAYS):
            at = q * WAYS + way
            to = peer(q, 1, way)
            if to is None:
                code1_got[at] = code1[at]
            else:
                send(code1.at[at], code1_got.at[at], c1_send.at[at], c1_recv.at[at], to)
        hop1_rows(q)

    load_cent.wait()

    def norms(i, carry):
        rows = pl.ds(pl.multiple_of(i * 128, 128), 128)
        wide = cent[rows, :].astype(F32)
        half_norm[rows, :] = 0.5 * jnp.sum(wide * wide, axis=1, keepdims=True)
        return carry

    lax.fori_loop(0, MESO_DEV * KF // 128, norms, 0)
    sums[...] = jnp.zeros_like(sums)
    counts[...] = jnp.zeros_like(counts)
    msum[...] = jnp.zeros_like(msum)
    mcount[...] = jnp.zeros_like(mcount)

    def hop2_codes(q):
        for way in range(WAYS):
            at = q * WAYS + way
            if peer(q, 1, way) is not None:
                arrived(code1_got.at[at], c1_send.at[at], c1_recv.at[at])
        tile = pl.ds(q * WAYS, WAYS)
        for way in range(WAYS):
            at = q * WAYS + way
            to = peer(q, 2, way)
            if to is None:
                code2[pl.ds(at * WAYS, WAYS)] = code1_got[tile]
            else:
                send(code1_got.at[tile], code2.at[pl.ds(at * WAYS, WAYS)], c2_send.at[at], c2_recv.at[at], to)

    def hop2_rows(q):
        for way in range(WAYS):
            at = q * WAYS + way
            if peer(q, 1, way) is not None:
                arrived(got1.at[q, pl.ds(way * BLOCK, BLOCK)], s1_send.at[at], s1_recv.at[at])
        mid[q] = dot(perm[...], got1[q]).astype(BF16)
        for way in range(WAYS):
            at = q * WAYS + way
            rows = pl.ds(way * BLOCK, BLOCK)
            to = peer(q, 2, way)
            if to is None:
                got2[q, rows, :] = mid[q, rows, :]
            else:
                send(mid.at[q, rows], got2.at[q, rows], s2_send.at[at], s2_recv.at[at], to)

    lane_of = iota((LANES, CHUNK_ROWS), 1)
    code_lane = div48(lane_of) * SLOTS + lane_of - 6 * div6(lane_of)
    code_pick = (iota((LANES, CHUNK_ROWS), 0) == code_lane).astype(F32).astype(BF16)
    pair_hit = iota((WAYS * WAYS, CHUNK_ROWS), 0) == div6(iota((WAYS * WAYS, CHUNK_ROWS), 1))
    back_row = iota((CHUNK_ROWS, LANES), 0)
    back_pick = (iota((CHUNK_ROWS, LANES), 1) == back_row - 48 * div48(back_row)).astype(F32).astype(BF16)
    back_hit = iota((WAYS, CHUNK_ROWS), 0) == div48(iota((WAYS, CHUNK_ROWS), 1))
    eye = iota((128, 128), 0) == iota((128, 128), 1)

    def codes_of(q):
        tile = code2[pl.ds(q * WAYS * WAYS, WAYS * WAYS)].reshape(WAYS * WAYS, LANES).astype(I32)
        high = dot((tile >> 4).astype(F32).astype(BF16), code_pick)
        low = dot((tile & 15).astype(F32).astype(BF16), code_pick)
        high = jnp.sum(jnp.where(pair_hit, high, 0.0), axis=0, keepdims=True)
        low = jnp.sum(jnp.where(pair_hit, low, 0.0), axis=0, keepdims=True)
        return (high.astype(I32), low.astype(I32))

    def wait_chunk(q):
        for way in range(WAYS):
            at = q * WAYS + way
            if peer(q, 2, way) is not None:
                arrived(code2.at[pl.ds(at * WAYS, WAYS)], c2_send.at[at], c2_recv.at[at])
                arrived(got2.at[q, pl.ds(way * BLOCK, BLOCK)], s2_send.at[at], s2_recv.at[at])

    def add_meso(q, high):
        hot = (iota((MESO_DEV, CHUNK_ROWS), 0) == high).astype(F32)
        msum[...] += dot(hot.astype(BF16), got2[q])
        mcount[...] += jnp.sum(hot, axis=1, keepdims=True)

    def score(q, high):
        norm = jnp.concatenate(
            [
                jnp.sum(
                    jnp.where(eye, dot(got2[q, t : t + 128, :], got2[q, t : t + 128, :], NT), 0.0),
                    axis=0, keepdims=True,
                )
                for t in range(0, CHUNK_ROWS, 128)
            ],
            axis=1,
        )

        def block(i, best):
            rows = pl.ds(pl.multiple_of(i * 256, 256), 256)
            cross = dot(cent[rows, :], got2[q], NT) - half_norm[rows, :]
            for t in range(256 // KF):
                top = jnp.max(cross[t * KF : (t + 1) * KF], axis=0, keepdims=True)
                best = jnp.where(high == i * (256 // KF) + t, top, best)
            return best

        best = lax.fori_loop(0, MESO_DEV * KF // 256, block, jnp.zeros((1, CHUNK_ROWS), F32))
        near = jnp.where(high >= 0, (norm - 2.0 * best) * (1.0 / D), 0.0)
        spread = sum(dot(part, back_pick) for part in split3(jnp.where(back_hit, near, 0.0)))
        for way in range(WAYS):
            at = q * WAYS + way
            ret1[at] = spread[way : way + 1, :]
            to = peer_back(q, 2, way)
            if to is None:
                ret1_got[at] = ret1[at]
            else:
                send(ret1.at[at], ret1_got.at[at], r1_send.at[at], r1_recv.at[at], to)

    def add_fine(q, high, low):
        code = (high << 4) + low

        def block(i, carry):
            rows = pl.ds(pl.multiple_of(i * 128, 128), 128)
            hot = (iota((128, CHUNK_ROWS), 0) + i * 128 == code).astype(F32)
            sums[rows, :] += dot(hot.astype(BF16), got2[q])
            counts[rows, :] += jnp.sum(hot, axis=1, keepdims=True)
            return carry

        lax.fori_loop(0, MESO_DEV * FGROUP // 128, block, 0)

    def pass_back(q):
        for way in range(WAYS):
            at = q * WAYS + way
            if peer(q, 2, way) is not None:
                arrived(ret1_got.at[at], r1_send.at[at], r1_recv.at[at])
        tile = pl.ds(q * WAYS, WAYS)
        for way in range(WAYS):
            at = q * WAYS + way
            to = peer_back(q, 1, way)
            if to is None:
                ret2[pl.ds(at * WAYS, WAYS)] = ret1_got[tile]
            else:
                send(ret1_got.at[tile], ret2.at[pl.ds(at * WAYS, WAYS)], r2_send.at[at], r2_recv.at[at], to)

    def work(q):
        wait_chunk(q)
        high, low = codes_of(q)
        add_meso(q, high)
        score(q, high)
        add_fine(q, high, low)

    for q in ORDER:
        hop2_codes(q)
    hop2_rows(3)
    hop2_rows(0)
    hop2_rows(1)
    work(0)
    hop2_rows(2)
    pass_back(0)
    work(1)
    pass_back(1)
    work(2)
    pass_back(2)

    wait_chunk(3)
    high, low = codes_of(3)
    add_meso(3, high)
    part[:, 0:D] = msum[...]
    part[:, D : D + LANES] = jnp.broadcast_to(mcount[...], (MESO_DEV, LANES))
    for dx in range(1, NX):
        send(part, part_got.at[dx - 1], p_send.at[dx - 1], p_recv.at[dx - 1], xc_peer(dx * NC))
    score(3, high)
    add_fine(3, high, low)
    pass_back(3)

    load_old.wait()
    for dx in range(1, NX):
        arrived(part_got.at[dx - 1], p_send.at[dx - 1], p_recv.at[dx - 1])
    total = (part[...] + part_got[1]) + (part_got[0] + part_got[2])
    new_meso_ref[...] = (total[:, 0:D] + old[...]) / (total[:, D : D + 1] + 1.0)

    def finish(m, carry):
        here = pl.ds(pl.multiple_of(m * FGROUP, FGROUP), FGROUP)
        mine = pl.ds(pl.multiple_of(m * KF + x * FGROUP, FGROUP), FGROUP)
        shift = new_meso_ref[pl.ds(m, 1), :] - old[pl.ds(m, 1), :]
        top = sums[here, :] + (cent[mine, :].astype(F32) + shift)
        new_fine_ref[here, :] = top / (counts[here, :] + 1.0)
        return carry

    lax.fori_loop(0, MESO_DEV, finish, 0)

    for q in range(CHUNKS):
        for way in range(WAYS):
            at = q * WAYS + way
            if peer(q, 1, way) is not None:
                arrived(ret2.at[pl.ds(at * WAYS, WAYS)], r2_send.at[at], r2_recv.at[at])
    back = ret2[...].reshape(BINS, LANES)
    picked = sum(dot(part, bin_hot, TN) for part in split3(back))
    mine = iota((LANES, ROWS), 0) == hop1 * SLOTS + rank
    near_ref[...] = jnp.sum(jnp.where(mine, picked, 0.0), axis=0, keepdims=True)

    for copy in sent:
        copy.wait_send()


def body(vectors, meso_labels, fine_labels, meso_centroids, fine_centroids):
    vmem = pl.BlockSpec(memory_space=pltpu.VMEM)
    hbm = pl.BlockSpec(memory_space=pl.ANY)
    hops = CHUNKS * WAYS
    dma = pltpu.SemaphoreType.DMA
    near, new_meso, new_fine = pl.pallas_call(
        kernel,
        out_shape=(
            jax.ShapeDtypeStruct((1, ROWS), F32),
            jax.ShapeDtypeStruct((MESO_DEV, D), F32),
            jax.ShapeDtypeStruct((MESO_DEV * FGROUP, D), F32),
        ),
        in_specs=[vmem, vmem, hbm, hbm, hbm],
        out_specs=(vmem, vmem, vmem),
        scratch_shapes=[
            pltpu.VMEM((ROWS, D), BF16),
            pltpu.VMEM((MESO_DEV, D), F32),
            pltpu.VMEM((MESO_DEV * KF, D), BF16),
            pltpu.VMEM((MESO_DEV * KF, 1), F32),
            pltpu.VMEM((CHUNK_ROWS, CHUNK_ROWS), BF16),
            pltpu.VMEM((CHUNKS, CHUNK_ROWS, D), BF16),
            pltpu.VMEM((CHUNKS, CHUNK_ROWS, D), BF16),
            pltpu.VMEM((CHUNKS, CHUNK_ROWS, D), BF16),
            pltpu.VMEM((CHUNKS, CHUNK_ROWS, D), BF16),
            pltpu.VMEM((hops, 1, LANES), F32),
            pltpu.VMEM((hops, 1, LANES), F32),
            pltpu.VMEM((BINS, 1, LANES), F32),
            pltpu.VMEM((hops, 1, LANES), F32),
            pltpu.VMEM((hops, 1, LANES), F32),
            pltpu.VMEM((BINS, 1, LANES), F32),
            pltpu.VMEM((MESO_DEV * FGROUP, D), F32),
            pltpu.VMEM((MESO_DEV * FGROUP, 1), F32),
            pltpu.VMEM((MESO_DEV, D), F32),
            pltpu.VMEM((MESO_DEV, 1), F32),
            pltpu.VMEM((MESO_DEV, D + LANES), F32),
            pltpu.VMEM((NX - 1, MESO_DEV, D + LANES), F32),
            dma((3,)),
        ]
        + [dma((hops,)) for _ in range(12)]
        + [dma((NX - 1,)), dma((NX - 1,))],
        compiler_params=pltpu.CompilerParams(
            collective_id=0, has_side_effects=True, vmem_limit_bytes=56 * 2**20
        ),
    )(
        meso_labels.reshape(1, ROWS),
        fine_labels.reshape(1, ROWS),
        vectors,
        meso_centroids,
        fine_centroids.reshape(MESO_DEV * KF, D),
    )
    return (near.reshape(ROWS), new_meso, new_fine.reshape(MESO_DEV, FGROUP, D))


def solution(mesh):
    return jax.shard_map(
        body,
        mesh=mesh,
        in_specs=(
            P(("dp", "owner"), None),
            P(("dp", "owner")),
            P(("dp", "owner")),
            P("owner", None),
            P("owner", None, None),
        ),
        out_specs=(P(("dp", "owner")), P("owner", None), P("owner", "dp", None)),
        check_vma=False,
    )
```

time: 281 us -> 121 us (0.43)
  waiting for transfers between devices: 127 us -> 0 us
  Pallas kernels: 0 us -> 110 us
  local copies, waits for them, and re-layouts: 48.7 us -> 7.26 us
  starting transfers between devices: 33.2 us -> 0 us
  blocking collectives: 22.5 us -> 0 us
  matrix products: 19.6 us -> 0 us
  other arithmetic: 15.1 us -> 1.29 us
  between operations: 14 us -> 0.64 us
    pallas_call x0 -> x1, Pallas kernels: none -> 110 us  [body(): pl.pallas_call(kernel, out_shape=(jax.ShapeDtypeStruct((1, ROWS), F32), j...]
    all_to_all x3 -> x0, waiting for transfers between devices: 78.4 us -> none  [the longest x1 69.7 us: body(): lax.all_to_all(packed, 'owner', split_axis=0, concat_axis=0, tiled=True)]
    reduce_scatter x2 -> x0, waiting for transfers between devices: 48.3 us -> none  [the longest x1 48.3 us: body(): lax.psum_scatter(all_sums.reshape(meso_dev, fine_count, feat_width), 'dp'...]
    all_to_all x3 -> x0, starting transfers between devices: 32.9 us -> none  [the longest x1 12.1 us: body(): lax.all_to_all(packed_codes, 'owner', split_axis=0, concat_axis=0, tiled=...]
    reshape x8 -> x2, local copies, waits for them, and re-layouts: 24 us -> 2.53 us  [the longest x1 1.27 us: body(): meso_labels.reshape(1, ROWS)]
    dot_general x2 -> x0, matrix products: 19.6 us -> none  [the longest x1 10.7 us: nearest_of(): lax.dot_general(flat_rows, centroid_table, (((1,), (1,)), ((), ())), pref...]
    all_gather x1 -> x0, blocking collectives: 12 us -> none  [body(): new_meso = lax.all_gather(new_share, 'dp', axis=1, tiled=True)]
    scatter x2 -> x0, local copies, waits for them, and re-layouts: 11 us -> none  [the longest x1 7.64 us: body(): jnp.zeros((bin_total * slot_count, feat_width), jnp.bfloat16).at[slot_index]]
  transfers between devices with their start and end apart: 6 -> 0, of which waited for: 3 -> 0; matrix products, arithmetic and copies ran while one was open for 25% -> 0% of each run, Pallas kernels for 0% -> 0%
where the time goes in v1:
time: 121 us; the launch traced here: 119 us
  Pallas kernels  110 us (91%)
  local copies, waits for them, and re-layouts  7.26 us (6%)
  other arithmetic  1.29 us (1%)
    pallas_call x1, Pallas kernels, body(): pl.pallas_call(kernel, out_shape=(jax.ShapeDtypeStruct((1, ROWS), F32), j...  110 us
    unnamed x2, local copies, waits for them, and re-layouts  4.73 us

profile of v1, /device:TPU:8, one launch (start us, length us, event | category | flops | bytes accessed | tf_op | source)
XLA Modules:
  0.0 118.8 jit_solution(764653190064158355)
XLA Ops:
  0.6 1.3 %reshape.21.meso_ref = s32[1,768]{1,0:T(1,128)} reshape(s32[768]{0:T(1024)} %param.6) | data formatting | bytes 6144 | tf_op jit(solution)/shard_map/reshape | solution.py:416
  1.9 1.3 %reshape.22.fine_ref = s32[1,768]{1,0:T(1,128)} reshape(s32[768]{0:T(1024)} %param.7) | data formatting | bytes 6144 | tf_op jit(solution)/shard_map/reshape | solution.py:417
  3.2 109.6 %shard_map.76 = (f32[1,768]{1,0:T(1,128)}, f32[32,1024]{1,0:T(8,128)}, f32[512,1024]{1,0:T(8,128)}) custom-call(s32[1,768]{1,0:T(1,128)} %reshape.21.meso_ref, s32[1,768]{1,0:T(1,128)} %reshape.22.fine_ref, bf16[768,1024]{1,0:T(8,128)(2,1)} %vec_hbm.1, f32[32,1024]{1,0:T(8,128)} %old_hbm.1, bf16[2048,1024]{1,0:T(8,128)(2,1)} %bitcast.2), custom_call_target="tpu_custom_call" | custom-call | tf_op jit(solution)/shard_map/pallas_call | solution.py:377
  112.8 1.3 %reduce = f32[768]{0:T(1024)} reduce(f32[1,768]{1,0:T(1,128)} %get-tuple-element.6, f32[]{:T(128)} %constant.2), dimensions={0}, to_apply=%get-tuple-element.6.reduce_sub_computation | reduce | bytes 6148 | tf_op jit(solution)/shard_map/pallas_call | solution.py:377
  114.1 1.6 %copy.10 = f32[32,1024]{1,0:T(8,128)} copy(f32[32,1024]{1,0:T(8,128)} %get-tuple-element.13) | data formatting | bytes 262144
  115.7 3.2 %copy.11 = f32[32,16,1024]{2,1,0:T(8,128)} copy(f32[32,16,1024]{2,1,0:T(8,128)} %bitcast.3) | data formatting | bytes 4194304

commit v2 on v0

v2 whole, which is shorter than its diff:
```python
import jax
import jax.numpy as jnp
from jax import lax
from jax.experimental import pallas as pl
from jax.experimental.pallas import tpu as pltpu
from jax.sharding import PartitionSpec as P

MESH = pl.DeviceIdType.MESH
D = 1024
ROWS = 768
KF = 64
MESO_DEV = 32
FGROUP = 16
SLOTS = 6
NX, NY, NZ, NC = 4, 4, 8, 2
CHUNKS = NY
WAYS = 8
BLOCK = WAYS * SLOTS
CHUNK_ROWS = WAYS * BLOCK
BINS = CHUNKS * WAYS * WAYS
LANES = 128
SHARE = MESO_DEV // NX
SPLIT = 2
LATE = CHUNKS - SPLIT
EARLY = SPLIT * WAYS
LATER = LATE * WAYS
PAIRS = WAYS * WAYS
HALF = CHUNK_ROWS // 2

F32, BF16, I32 = jnp.float32, jnp.bfloat16, jnp.int32
NT = (((1,), (1,)), ((), ()))
TN = (((0,), (0,)), ((), ()))


def iota(shape, dim):
    return lax.broadcasted_iota(I32, shape, dim)


def div6(v):
    return (v * 10923) >> 16


def div48(v):
    return div6(v >> 3)


def split3(v):
    first = v.astype(BF16)
    rest = v - first.astype(F32)
    second = rest.astype(BF16)
    third = (rest - second.astype(F32)).astype(BF16)
    return (first, second, third)


def dot(a, b, dims=(((1,), (0,)), ((), ()))):
    return lax.dot_general(a, b, dims, preferred_element_type=F32)


def each(low, high, step):
    def body(i, carry):
        step(i)
        return carry

    lax.fori_loop(low, high, body, 0)


def kernel(
    meso_hbm, fine_hbm, vec_hbm, old_hbm, cent_hbm,
    near_ref, new_meso_ref, new_fine_ref,
    meso_ref, fine_ref, vec, old, cent, half_norm, perm, packed, got1, mid, got2,
    code1, code1_got, code2, last1, last1_got, last_mid, last2,
    ret1, ret1_got, ret_mid, back1, back1_got, ret2,
    sums, counts, msum, mcount, part, part_got, new_part, new_all,
    hot_ref, bin_hot, bin_ref, rank_ref, slot_ref,
    load_sem, s1_send, s1_recv, s2_send, s2_recv, c1_send, c1_recv, c2_send, c2_recv,
    r1_send, r1_recv, r2_send, r2_recv, p_send, p_recv, n_send, n_recv, gate,
):
    x = lax.axis_index("dp")
    own = lax.axis_index("owner")
    y, z, c = lax.div(own, 16), lax.rem(lax.div(own, 2), 8), lax.rem(own, 2)

    def yz_peer(dy, dz):
        return (x, (lax.rem(y + dy, NY) * NZ + lax.rem(z + dz, NZ)) * NC + c)

    def xc_peer(j):
        return (lax.rem(x + lax.div(j, NC), NX), (y * NZ + z) * NC + lax.rem(c + lax.rem(j, NC), NC))

    def xc_back(j):
        return (lax.rem(x + NX - lax.div(j, NC), NX), (y * NZ + z) * NC + lax.rem(c + lax.rem(j, NC), NC))

    def yz_back(dy, dz):
        return yz_peer(NY - dy, NZ - dz)

    def near_z(way):
        odd = lax.rem(way, 2)
        return lax.rem(odd * lax.div(way + 1, 2) + (1 - odd) * lax.div(2 * NZ - way, 2), NZ)

    def start_of(q):
        return lax.div(SPLIT - q, SPLIT)

    def link(src, dst, send_sem, recv_sem, device):
        return pltpu.make_async_remote_copy(
            src_ref=src, dst_ref=dst, send_sem=send_sem, recv_sem=recv_sem,
            device_id=device, device_id_type=MESH,
        )

    here = (x, own)

    def arrived(dst, send_sem, recv_sem):
        link(dst, dst, send_sem, recv_sem, here).wait_recv()

    def left(src, send_sem, recv_sem):
        link(src, src, send_sem, recv_sem, here).wait_send()

    def block(way):
        return pl.ds(pl.multiple_of(way * BLOCK, BLOCK), BLOCK)

    def ways(at):
        return pl.ds(at * WAYS, WAYS)

    barrier = pltpu.get_barrier_semaphore()

    def greet(device):
        pl.semaphore_signal(barrier, 1, device_id=device, device_id_type=MESH)

    each(1, NZ, lambda dz: greet(yz_peer(0, dz)))
    each(1, NY, lambda dy: greet(yz_peer(dy, 0)))
    each(1, WAYS, lambda j: greet(xc_peer(j)))
    greeted = NZ + NY + WAYS - 3

    load_meso = pltpu.make_async_copy(meso_hbm, meso_ref, load_sem.at[3])
    load_fine = pltpu.make_async_copy(fine_hbm, fine_ref, load_sem.at[4])
    load_vec = pltpu.make_async_copy(vec_hbm, vec, load_sem.at[0])
    load_cent = pltpu.make_async_copy(cent_hbm, cent, load_sem.at[1])
    load_old = pltpu.make_async_copy(old_hbm, old, load_sem.at[2])
    for load in (load_meso, load_fine, load_vec, load_cent, load_old):
        load.start()

    load_meso.wait()
    load_fine.wait()
    meso = meso_ref[...].reshape(1, ROWS)
    fine = fine_ref[...].reshape(1, ROWS)
    to = meso >> 5
    dy = ((to >> 4) - y) & 3
    dz = (((to >> 1) & 7) - z) & 7
    way = ((((fine >> 4) - x) & 3) << 1) + ((to - c) & 1)
    z_near = jnp.where(dz <= 4, jnp.maximum(2 * dz - 1, 0), 2 * (NZ - dz))
    is_last = dy >= SPLIT
    hop1 = jnp.where(is_last, way, dz)
    hop2 = jnp.where(is_last, z_near, way)
    first = (dy << 3) + hop1
    bin_of = (first << 3) + hop2
    bin_ref[...] = bin_of

    def bin_rows(i):
        rows = pl.ds(pl.multiple_of(i * 64, 64), 64)
        bin_hot[rows, :] = (iota((64, ROWS), 0) + i * 64 == bin_of).astype(F32).astype(BF16)

    each(0, BINS // 64, bin_rows)

    def ranks(i):
        lanes = pl.ds(pl.multiple_of(i * LANES, LANES), LANES)
        before = (iota((ROWS, LANES), 0) < iota((ROWS, LANES), 1) + i * LANES).astype(F32).astype(BF16)
        ahead = dot(bin_hot[...], before)
        mine = iota((BINS, LANES), 0) == bin_ref[:, lanes]
        rank_ref[:, lanes] = jnp.sum(jnp.where(mine, ahead, 0.0), axis=0, keepdims=True).astype(I32)

    each(0, ROWS // LANES, ranks)
    rank = rank_ref[...]
    slot_ref[...] = bin_of * SLOTS + rank

    meso_code = ((meso & 31) + 1).astype(F32)
    fine_code = (fine & 15).astype(F32)

    def code_rows(hit, lane):
        hot = (iota((LANES, ROWS), 0) == lane).astype(F32).astype(BF16)
        high = jnp.where(hit, meso_code, 0.0).astype(BF16)
        low = jnp.where(hit, fine_code, 0.0).astype(BF16)
        return 16.0 * dot(high, hot, NT) + dot(low, hot, NT)

    codes = code_rows(iota((EARLY, ROWS), 0) == first, hop2 * SLOTS + rank)
    for r in range(EARLY):
        code1[r] = codes[r : r + 1, :]
    codes = code_rows(iota((LATE * PAIRS, ROWS), 0) + SPLIT * PAIRS == bin_of, hop1 * SLOTS + rank)
    for r in range(LATE * PAIRS):
        last1[r] = codes[r : r + 1, :]

    load_vec.wait()

    def pack(q):
        def hot_rows(i):
            rows = pl.ds(pl.multiple_of(i * 64, 64), 64)
            at = iota((64, ROWS), 0) + (q * CHUNK_ROWS + i * 64)
            hot_ref[rows, :] = (at == slot_ref[...]).astype(F32).astype(BF16)

        def columns(i):
            lanes = pl.ds(pl.multiple_of(i * 256, 256), 256)
            packed[q, :, lanes] = dot(hot_ref[...], vec[:, lanes]).astype(BF16)

        each(0, CHUNK_ROWS // 64, hot_rows)
        each(0, D // 256, columns)

    def leave_late(q):
        late = q - SPLIT

        def code(way):
            at = late * WAYS + way
            link(last1.at[ways(at)], last1_got.at[ways(at)], c1_send.at[EARLY + at], c1_recv.at[EARLY + at], xc_peer(way)).start()

        def rows(way):
            at = q * WAYS + way
            link(packed.at[q, block(way)], got1.at[q, block(way)], s1_send.at[at], s1_recv.at[at], xc_peer(way)).start()

        last1_got[ways(late * WAYS)] = last1[ways(late * WAYS)]
        got1[q, 0:BLOCK, :] = packed[q, 0:BLOCK, :]
        each(1, WAYS, code)
        each(1, WAYS, rows)

    def leave_early(q):
        def code(way):
            at = q * WAYS + way
            link(code1.at[at], code1_got.at[at], c1_send.at[at], c1_recv.at[at], yz_peer(q, way)).start()

        def rows(way):
            at = q * WAYS + way
            link(packed.at[q, block(way)], got1.at[q, block(way)], s1_send.at[at], s1_recv.at[at], yz_peer(q, way)).start()

        each(start_of(q), WAYS, code)
        each(start_of(q), WAYS, rows)

    def pack_next(n):
        pack(lax.rem(n + SPLIT, CHUNKS))

    def signal(dy):
        pl.semaphore_signal(gate, 1, device_id=yz_peer(dy, 0), device_id_type=MESH)

    each(0, LATE + 1, pack_next)
    pl.semaphore_wait(barrier, greeted)
    code1_got[0] = code1[0]
    got1[0, 0:BLOCK, :] = packed[0, 0:BLOCK, :]
    leave_late(SPLIT)
    leave_early(0)
    each(1, NY, signal)
    each(SPLIT + 1, CHUNKS, leave_late)
    each(LATE + 1, CHUNKS, pack_next)
    pl.semaphore_wait(gate, NY - 1)
    each(1, SPLIT, leave_early)

    def perm_rows(i):
        rows = pl.ds(pl.multiple_of(i * 64, 64), 64)
        out_row = iota((64, CHUNK_ROWS), 0) + i * 64
        in_row = iota((64, CHUNK_ROWS), 1)
        out_pair, in_pair = div6(out_row), div6(in_row)
        swapped = ((out_pair & 7) << 3) + (out_pair >> 3)
        hit = in_row - 6 * in_pair + 6 * swapped == out_row - 6 * out_pair + 6 * in_pair
        perm[rows, :] = hit.astype(F32).astype(BF16)

    each(0, CHUNK_ROWS // 64, perm_rows)

    def regroup(q):
        def columns(i):
            lanes = pl.ds(pl.multiple_of(i * 256, 256), 256)
            mid[q, :, lanes] = dot(perm[...], got1[q, :, lanes]).astype(BF16)

        each(0, D // 256, columns)

    def pass_late(q):
        late = q - SPLIT

        def codes(way):
            at = late * WAYS + way
            arrived(last1_got.at[ways(at)], c1_send.at[EARLY + at], c1_recv.at[EARLY + at])

        def rows(way):
            at = q * WAYS + way
            arrived(got1.at[q, block(way)], s1_send.at[at], s1_recv.at[at])

        def codes_on(way):
            at = late * WAYS + way
            device = yz_peer(q, near_z(way))
            link(last_mid.at[at], last2.at[at], c2_send.at[EARLY + at], c2_recv.at[EARLY + at], device).start()

        def rows_on(way):
            at = q * WAYS + way
            device = yz_peer(q, near_z(way))
            link(mid.at[q, block(way)], got2.at[q, block(way)], s2_send.at[at], s2_recv.at[at], device).start()

        each(1, WAYS, codes)
        last_mid[ways(late)] = sum(last1_got[pl.ds(late * PAIRS + way * WAYS, WAYS)] for way in range(WAYS))
        each(0, WAYS, codes_on)
        each(1, WAYS, rows)
        regroup(q)
        each(0, WAYS, rows_on)

    each(SPLIT, CHUNKS, pass_late)

    load_cent.wait()

    def norms(i):
        rows = pl.ds(pl.multiple_of(i * 32, 32), 32)
        wide = cent[rows, :].astype(F32)
        half_norm[rows, :] = 0.5 * jnp.sum(wide * wide, axis=1, keepdims=True)

    each(0, MESO_DEV * KF // 32, norms)

    def clear(i):
        rows = pl.ds(pl.multiple_of(i * 32, 32), 32)
        sums[rows, :] = jnp.zeros((32, D), F32)

    each(0, MESO_DEV * FGROUP // 32, clear)
    counts[...] = jnp.zeros_like(counts)
    msum[...] = jnp.zeros_like(msum)
    mcount[...] = jnp.zeros_like(mcount)

    def codes_from(tile, hit, pick):
        tile = tile.astype(I32)
        high = dot((tile >> 4).astype(F32).astype(BF16), pick)
        low = dot((tile & 15).astype(F32).astype(BF16), pick)
        high = jnp.sum(jnp.where(hit, high, 0.0), axis=0, keepdims=True)
        low = jnp.sum(jnp.where(hit, low, 0.0), axis=0, keepdims=True)
        return (high.astype(I32) - 1, low.astype(I32))

    def add_meso(members, high):
        hot = (iota((MESO_DEV, members.shape[0]), 0) == high).astype(F32)
        msum[...] += dot(hot.astype(BF16), members)
        mcount[...] += jnp.sum(hot, axis=1, keepdims=True)

    def nearest(members, high):
        size = members.shape[0]
        step = LANES if size % LANES == 0 else size
        eye = iota((step, step), 0) == iota((step, step), 1)
        norm = jnp.concatenate(
            [
                jnp.sum(
                    jnp.where(eye, dot(members[t : t + step], members[t : t + step], NT), 0.0), axis=0, keepdims=True
                )
                for t in range(0, size, step)
            ],
            axis=1,
        )

        best = jnp.zeros((1, size), F32)
        for i in range(0, MESO_DEV * KF, 1024):
            cross = dot(cent[i : i + 1024, :], members, NT) - half_norm[i : i + 1024, :]
            for t in range(0, 1024, KF):
                top = jnp.max(cross[t : t + KF], axis=0, keepdims=True)
                best = jnp.where(high == (i + t) // KF, top, best)
        return jnp.where(high >= 0, (norm - 2.0 * best) * (1.0 / D), 0.0)

    def add_fine(members, high, low):
        code = (high << 4) + low
        size = members.shape[0]

        def step(i):
            rows = pl.ds(pl.multiple_of(i * 128, 128), 128)
            hot = (iota((128, size), 0) + i * 128 == code).astype(F32)
            sums[rows, :] += dot(hot.astype(BF16), members)
            counts[rows, :] += jnp.sum(hot, axis=1, keepdims=True)

        each(0, MESO_DEV * FGROUP // 128, step)

    def spread_of(near, hit, pick):
        return sum(dot(piece, pick, NT) for piece in split3(jnp.where(hit, near, 0.0)))

    def pass_on(q):
        def codes(way):
            at = q * WAYS + way
            arrived(code1_got.at[at], c1_send.at[at], c1_recv.at[at])

        def rows(way):
            at = q * WAYS + way
            arrived(got1.at[q, block(way)], s1_send.at[at], s1_recv.at[at])

        def codes_on(way):
            at = q * WAYS + way
            link(code1_got.at[ways(q)], code2.at[ways(at)], c2_send.at[at], c2_recv.at[at], xc_peer(way)).start()

        def rows_on(way):
            at = q * WAYS + way
            link(mid.at[q, block(way)], got2.at[q, block(way)], s2_send.at[at], s2_recv.at[at], xc_peer(way)).start()

        each(start_of(q), WAYS, codes)
        code2[ways(q * WAYS)] = code1_got[ways(q)]
        each(1, WAYS, codes_on)
        each(start_of(q), WAYS, rows)
        regroup(q)
        got2[q, 0:BLOCK, :] = mid[q, 0:BLOCK, :]
        each(1, WAYS, rows_on)

    def work(q):
        def codes(way):
            at = q * WAYS + way
            arrived(code2.at[ways(at)], c2_send.at[at], c2_recv.at[at])

        def rows(way):
            at = q * WAYS + way
            arrived(got2.at[q, block(way)], s2_send.at[at], s2_recv.at[at])

        row = iota((LANES, CHUNK_ROWS), 1)
        pick = (iota((LANES, CHUNK_ROWS), 0) == div48(row) * SLOTS + row - 6 * div6(row)).astype(F32).astype(BF16)
        hit = iota((WAYS * WAYS, CHUNK_ROWS), 0) == div6(iota((WAYS * WAYS, CHUNK_ROWS), 1))
        each(1, WAYS, codes)
        tile = code2[pl.ds(q * WAYS * WAYS, WAYS * WAYS)].reshape(WAYS * WAYS, LANES)
        high, low = codes_from(tile, hit, pick)
        each(1, WAYS, rows)
        members = got2[q]
        spread = spread_of(nearest(members, high), hit, pick)
        for r in range(WAYS * WAYS):
            ret1[q * WAYS * WAYS + r] = spread[r : r + 1, :]
        ret1_got[ways(q * WAYS)] = ret1[ways(q * WAYS)]

        def back(way):
            at = q * WAYS + way
            link(ret1.at[ways(at)], ret1_got.at[ways(at)], r1_send.at[at], r1_recv.at[at], xc_back(way)).start()

        each(1, WAYS, back)
        add_meso(members, high)
        add_fine(members, high, low)

    def pass_back(q):
        def wait(way):
            at = q * WAYS + way
            arrived(ret1_got.at[ways(at)], r1_send.at[at], r1_recv.at[at])

        def back(way):
            at = q * WAYS + way
            link(ret_mid.at[at], ret2.at[at], r2_send.at[at], r2_recv.at[at], yz_back(q, way)).start()

        each(1, WAYS, wait)
        ret_mid[ways(q)] = sum(ret1_got[pl.ds((q * WAYS + way) * WAYS, WAYS)] for way in range(WAYS))
        each(start_of(q), WAYS, back)

    def turn(i):
        pass_on(i)

        @pl.when(i > 0)
        def _():
            pass_back(i - 1)

        work(i)

    each(0, SPLIT, turn)
    load_old.wait()

    def late_codes(at):
        arrived(last2.at[at], c2_send.at[EARLY + at], c2_recv.at[EARLY + at])

    def late_half(n):
        q = SPLIT + lax.div(n, 2)
        h = lax.rem(n, 2)
        late = lax.div(n, 2)
        row = iota((LANES, HALF), 1) + h * HALF
        pick = (iota((LANES, HALF), 0) == row - 48 * div48(row)).astype(F32).astype(BF16)
        hit = iota((WAYS, HALF), 0) == div48(iota((WAYS, HALF), 1) + h * HALF)

        @pl.when(h == 0)
        def _():
            each(late * WAYS, late * WAYS + WAYS, late_codes)

        high, low = codes_from(last2[ways(late)].reshape(WAYS, LANES), hit, pick)

        def rows(way):
            at = q * WAYS + way
            arrived(got2.at[q, block(way)], s2_send.at[at], s2_recv.at[at])

        start = h * (WAYS // 2)
        each(start, start + WAYS // 2, rows)
        members = got2[q, pl.ds(pl.multiple_of(h * HALF, HALF), HALF), :]
        add_meso(members, high)

        @pl.when(n == 2 * LATE - 1)
        def _():
            part[:, 0:D] = msum[...]
            part[:, D : D + LANES] = jnp.broadcast_to(mcount[...], (MESO_DEV, LANES))

            def share_out(dx):
                share = pl.ds(pl.multiple_of(lax.rem(x + dx, NX) * SHARE, SHARE), SHARE)
                device = xc_peer(dx * NC)
                link(part.at[share], part_got.at[dx - 1], p_send.at[dx - 1], p_recv.at[dx - 1], device).start()

            each(1, NX, share_out)

        spread = spread_of(nearest(members, high), hit, pick)
        for r in range(WAYS):
            @pl.when(h == r // (WAYS // 2))
            def _():
                back1[late * WAYS + r] = spread[r : r + 1, :]

        def back(way):
            at = late * WAYS + way
            device = yz_back(q, near_z(way))
            link(back1.at[at], back1_got.at[at], r1_send.at[EARLY + at], r1_recv.at[EARLY + at], device).start()

        each(start, start + WAYS // 2, back)
        add_fine(members, high, low)

        @pl.when(n == 1)
        def _():
            pass_back(SPLIT - 1)

    each(0, 2 * LATE, late_half)
    ret2[0] = ret_mid[0]

    def begin(m):
        rows = pl.ds(pl.multiple_of(m * FGROUP, FGROUP), FGROUP)
        mine = pl.ds(pl.multiple_of(m * KF + x * FGROUP, FGROUP), FGROUP)
        sums[rows, :] += cent[mine, :].astype(F32) - old[pl.ds(m, 1), :]

    each(0, MESO_DEV, begin)

    each(1, NX, lambda dx: arrived(part_got.at[dx - 1], p_send.at[dx - 1], p_recv.at[dx - 1]))
    share = pl.ds(pl.multiple_of(x * SHARE, SHARE), SHARE)
    total = (part[share, :] + part_got[1]) + (part_got[0] + part_got[2])
    new_part[...] = (total[:, 0:D] + old[share, :]) / (total[:, D : D + 1] + 1.0)

    def hand_out(dx):
        link(new_part, new_all.at[dx - 1], n_send.at[dx - 1], n_recv.at[dx - 1], xc_peer(dx * NC)).start()

    each(1, NX, hand_out)
    new_meso_ref[share, :] = new_part[...]

    def late_back(late):
        def wait(way):
            at = late * WAYS + way
            arrived(back1_got.at[at], r1_send.at[EARLY + at], r1_recv.at[EARLY + at])

        def back(way):
            at = late * WAYS + way
            link(
                back1_got.at[ways(late)], ret2.at[pl.ds(EARLY + at * WAYS, WAYS)], r2_send.at[EARLY + at], r2_recv.at[EARLY + at], xc_back(way)
            ).start()

        each(0, WAYS, wait)
        ret2[pl.ds(EARLY + late * PAIRS, WAYS)] = back1_got[ways(late)]
        each(1, WAYS, back)

    each(0, LATE, late_back)

    for dx in range(1, NX):
        arrived(new_all.at[dx - 1], n_send.at[dx - 1], n_recv.at[dx - 1])
        share = pl.ds(pl.multiple_of(lax.rem(x + NX - dx, NX) * SHARE, SHARE), SHARE)
        new_meso_ref[share, :] = new_all[dx - 1]

    def finish(m):
        rows = pl.ds(pl.multiple_of(m * FGROUP, FGROUP), FGROUP)
        new_fine_ref[rows, :] = (sums[rows, :] + new_meso_ref[pl.ds(m, 1), :]) / (counts[rows, :] + 1.0)

    each(0, MESO_DEV, finish)

    from_row = jnp.where(is_last, bin_of - SPLIT * PAIRS + EARLY, first)
    row_hot = (iota((EARLY + LATE * PAIRS, ROWS), 0) == from_row).astype(F32).astype(BF16)
    mine = iota((LANES, ROWS), 0) == jnp.where(is_last, hop1, hop2) * SLOTS + rank
    each(1, EARLY, lambda at: arrived(ret2.at[at], r2_send.at[at], r2_recv.at[at]))

    def late_returned(n):
        late = lax.div(n, WAYS - 1)
        at = late * WAYS + 1 + lax.rem(n, WAYS - 1)
        arrived(ret2.at[pl.ds(EARLY + at * WAYS, WAYS)], r2_send.at[EARLY + at], r2_recv.at[EARLY + at])

    each(0, LATE * (WAYS - 1), late_returned)
    returned = ret2[...].reshape(EARLY + LATE * PAIRS, LANES)
    picked = sum(dot(piece, row_hot, TN) for piece in split3(returned))
    near_ref[...] = jnp.sum(jnp.where(mine, picked, 0.0), axis=0, keepdims=True).reshape(ROWS)

    def early_left(at):
        q = lax.div(at, WAYS)
        way = lax.rem(at, WAYS)
        left(packed.at[q, block(way)], s1_send.at[at], s1_recv.at[at])
        left(code1.at[at], c1_send.at[at], c1_recv.at[at])
        left(ret_mid.at[at], r2_send.at[at], r2_recv.at[at])

    def early_left2(at):
        q = lax.div(at, WAYS - 1)
        way = lax.rem(at, WAYS - 1) + 1
        at = q * WAYS + way
        left(mid.at[q, block(way)], s2_send.at[at], s2_recv.at[at])
        left(code1_got.at[ways(q)], c2_send.at[at], c2_recv.at[at])
        left(ret1.at[ways(at)], r1_send.at[at], r1_recv.at[at])

    def late_left(n):
        late = lax.div(n, WAYS - 1)
        way = lax.rem(n, WAYS - 1) + 1
        at = EARLY + late * WAYS + way
        left(packed.at[SPLIT + late, block(way)], s1_send.at[at], s1_recv.at[at])
        left(last1.at[ways(late * WAYS + way)], c1_send.at[at], c1_recv.at[at])
        left(back1_got.at[ways(late)], r2_send.at[at], r2_recv.at[at])

    def late_left2(n):
        late = lax.div(n, WAYS)
        way = lax.rem(n, WAYS)
        at = EARLY + n
        left(mid.at[SPLIT + late, block(way)], s2_send.at[at], s2_recv.at[at])
        left(last_mid.at[n], c2_send.at[at], c2_recv.at[at])
        left(back1.at[n], r1_send.at[at], r1_recv.at[at])

    def meso_left(dx):
        left(part_got.at[dx], p_send.at[dx], p_recv.at[dx])
        left(new_part, n_send.at[dx], n_recv.at[dx])

    each(1, EARLY, early_left)
    each(0, SPLIT * (WAYS - 1), early_left2)
    each(0, LATE * (WAYS - 1), late_left)
    each(0, LATER, late_left2)
    each(0, NX - 1, meso_left)


def body(vectors, meso_labels, fine_labels, meso_centroids, fine_centroids):
    hbm = pl.BlockSpec(memory_space=pl.ANY)
    vmem = pl.BlockSpec(memory_space=pltpu.VMEM)
    hops = CHUNKS * WAYS
    dma = pltpu.SemaphoreType.DMA
    outs = (((ROWS,), F32), ((MESO_DEV, D), F32), ((MESO_DEV * FGROUP, D), F32))

    def row(count):
        return pltpu.VMEM((count, 1, LANES), F32)

    near, new_meso, new_fine = pl.pallas_call(
        kernel,
        out_shape=tuple(pltpu.VMEM(*out) for out in outs),
        in_specs=[hbm] * 5,
        out_specs=(vmem,) * 3,
        scratch_shapes=[
            pltpu.VMEM((ROWS,), I32),
            pltpu.VMEM((ROWS,), I32),
            pltpu.VMEM((ROWS, D), BF16),
            pltpu.VMEM((MESO_DEV, D), F32),
            pltpu.VMEM((MESO_DEV * KF, D), BF16),
            pltpu.VMEM((MESO_DEV * KF, 1), F32),
            pltpu.VMEM((CHUNK_ROWS, CHUNK_ROWS), BF16),
            pltpu.VMEM((CHUNKS, CHUNK_ROWS, D), BF16),
            pltpu.VMEM((CHUNKS, CHUNK_ROWS, D), BF16),
            pltpu.VMEM((CHUNKS, CHUNK_ROWS, D), BF16),
            pltpu.VMEM((CHUNKS, CHUNK_ROWS, D), BF16),
            row(EARLY), row(EARLY), row(EARLY * WAYS),
            row(LATE * PAIRS), row(LATE * PAIRS), row(LATER), row(LATER),
            row(EARLY * WAYS), row(EARLY * WAYS), row(EARLY),
            row(LATER), row(LATER), row(EARLY + LATE * PAIRS),
            pltpu.VMEM((MESO_DEV * FGROUP, D), F32),
            pltpu.VMEM((MESO_DEV * FGROUP, 1), F32),
            pltpu.VMEM((MESO_DEV, D), F32),
            pltpu.VMEM((MESO_DEV, 1), F32),
            pltpu.VMEM((MESO_DEV, D + LANES), F32),
            pltpu.VMEM((NX - 1, SHARE, D + LANES), F32),
            pltpu.VMEM((SHARE, D), F32),
            pltpu.VMEM((NX - 1, SHARE, D), F32),
            pltpu.VMEM((CHUNK_ROWS, ROWS), BF16),
            pltpu.VMEM((BINS, ROWS), BF16),
            pltpu.VMEM((1, ROWS), I32),
            pltpu.VMEM((1, ROWS), I32),
            pltpu.VMEM((1, ROWS), I32),
            dma((5,)),
        ]
        + [dma((hops,)) for _ in range(12)]
        + [dma((NX - 1,)) for _ in range(4)]
        + [pltpu.SemaphoreType.REGULAR],
        compiler_params=pltpu.CompilerParams(
            collective_id=0, has_side_effects=True, vmem_limit_bytes=61 * 2**20
        ),
    )(
        meso_labels,
        fine_labels,
        vectors,
        meso_centroids,
        fine_centroids.reshape(MESO_DEV * KF, D),
    )
    return (near, new_meso, new_fine.reshape(MESO_DEV, FGROUP, D))


def solution(mesh):
    return jax.shard_map(
        body,
        mesh=mesh,
        in_specs=(
            P(("dp", "owner"), None),
            P(("dp", "owner")),
            P(("dp", "owner")),
            P("owner", None),
            P("owner", None, None),
        ),
        out_specs=(P(("dp", "owner")), P("owner", None), P("owner", "dp", None)),
        check_vma=False,
    )
```

time: 281 us -> 110 us (0.39)
  waiting for transfers between devices: 127 us -> 0 us
  Pallas kernels: 0 us -> 105 us
  local copies, waits for them, and re-layouts: 48.7 us -> 2.57 us
  starting transfers between devices: 33.2 us -> 0 us
  blocking collectives: 22.5 us -> 0 us
  matrix products: 19.6 us -> 0 us
  other arithmetic: 15.1 us -> 0 us
  between operations: 14 us -> 0.64 us
    pallas_call x0 -> x1, Pallas kernels: none -> 105 us  [body(): pl.pallas_call(kernel, out_shape=tuple((pltpu.VMEM(*out) for out in outs)...]
    all_to_all x3 -> x0, waiting for transfers between devices: 78.4 us -> none  [the longest x1 69.7 us: body(): lax.all_to_all(packed, 'owner', split_axis=0, concat_axis=0, tiled=True)]
    reduce_scatter x2 -> x0, waiting for transfers between devices: 48.3 us -> none  [the longest x1 48.3 us: body(): lax.psum_scatter(all_sums.reshape(meso_dev, fine_count, feat_width), 'dp'...]
    all_to_all x3 -> x0, starting transfers between devices: 32.9 us -> none  [the longest x1 12.1 us: body(): lax.all_to_all(packed_codes, 'owner', split_axis=0, concat_axis=0, tiled=...]
    reshape x8 -> x0, local copies, waits for them, and re-layouts: 24 us -> none  [the longest x2 13 us: body(): packed = packed.reshape(owner_total, dp_total, slot_count, feat_width)]
    dot_general x2 -> x0, matrix products: 19.6 us -> none  [the longest x1 10.7 us: nearest_of(): lax.dot_general(flat_rows, centroid_table, (((1,), (1,)), ((), ())), pref...]
    all_gather x1 -> x0, blocking collectives: 12 us -> none  [body(): new_meso = lax.all_gather(new_share, 'dp', axis=1, tiled=True)]
    scatter x2 -> x0, local copies, waits for them, and re-layouts: 11 us -> none  [the longest x1 7.64 us: body(): jnp.zeros((bin_total * slot_count, feat_width), jnp.bfloat16).at[slot_index]]
  transfers between devices with their start and end apart: 6 -> 0, of which waited for: 3 -> 0; matrix products, arithmetic and copies ran while one was open for 25% -> 0% of each run, Pallas kernels for 0% -> 0%
where the time goes in v2:
time: 110 us; the launch traced here: 109 us
  Pallas kernels  105 us (95%)
  local copies, waits for them, and re-layouts  2.57 us (2%)
    pallas_call x1, Pallas kernels, body(): pl.pallas_call(kernel, out_shape=tuple((pltpu.VMEM(*out) for out in outs)...  105 us
    unnamed x3, local copies, waits for them, and re-layouts  2.57 us

profile of v2, /device:TPU:8, one launch (start us, length us, event | category | flops | bytes accessed | tf_op | source)
XLA Modules:
  0.0 108.6 jit_solution(2720596464923110439)
XLA Ops:
  0.6 105.4 %shard_map.76 = (f32[768]{0:T(1024)S(1)}, f32[32,1024]{1,0:T(8,128)S(1)}, f32[512,1024]{1,0:T(8,128)S(1)}) custom-call(s32[768]{0:T(1024)} %meso_hbm.1, s32[768]{0:T(1024)} %fine_hbm.1, bf16[768,1024]{1,0:T(8,128)(2,1)} %vec_hbm.1, f32[32,1024]{1,0:T(8,128)} %old_hbm.1, bf16[2048,1024]{1,0:T(8,128)(2,1)} %bitcast.3), custom_call_target="tpu_custom_call" | custom-call | tf_op jit(solution)/shard_map/pallas_call | solution.py:617
  106.0 0.6 copy.11
  106.6 0.7 copy.12
  107.3 1.3 %copy.13 = f32[32,16,1024]{2,1,0:T(8,128)} copy(f32[32,16,1024]{2,1,0:T(8,128)S(1)} %bitcast.2) | data formatting | bytes 4194304

commit v3 on v2

--- a/solution.py
+++ b/solution.py
@@ -69,9 +69,9 @@
     near_ref, new_meso_ref, new_fine_ref,
     meso_ref, fine_ref, vec, old, cent, half_norm, perm, packed, got1, mid, got2,
     code1, code1_got, code2, last1, last1_got, last_mid, last2,
-    ret1, ret1_got, ret_mid, back1, back1_got, ret2,
+    ret1, ret1_got, ret_mid, back1, ret2,
     sums, counts, msum, mcount, part, part_got, new_part, new_all,
-    hot_ref, bin_hot, bin_ref, rank_ref, slot_ref,
+    hot_ref, bin_hot, bin_ref, rank_ref, slot_ref, row_hot, inverse,
     load_sem, s1_send, s1_recv, s2_send, s2_recv, c1_send, c1_recv, c2_send, c2_recv,
     r1_send, r1_recv, r2_send, r2_recv, p_send, p_recv, n_send, n_recv, gate,
 ):
@@ -181,10 +181,6 @@
     codes = code_rows(iota((EARLY, ROWS), 0) == first, hop2 * SLOTS + rank)
     for r in range(EARLY):
         code1[r] = codes[r : r + 1, :]
-    codes = code_rows(iota((LATE * PAIRS, ROWS), 0) + SPLIT * PAIRS == bin_of, hop1 * SLOTS + rank)
-    for r in range(LATE * PAIRS):
-        last1[r] = codes[r : r + 1, :]
-
     load_vec.wait()
 
     def pack(q):
@@ -204,13 +200,13 @@
         late = q - SPLIT
 
         def code(way):
-            at = late * WAYS + way
-            link(last1.at[ways(at)], last1_got.at[ways(at)], c1_send.at[EARLY + at], c1_recv.at[EARLY + at], xc_peer(way)).start()
+            at = ways(late * WAYS + way)
+            link(last1.at[at], last1_got.at[at], c1_send.at[q], c1_recv.at[q], xc_peer(way)).start()
 
         def rows(way):
-            at = q * WAYS + way
-            link(packed.at[q, block(way)], got1.at[q, block(way)], s1_send.at[at], s1_recv.at[at], xc_peer(way)).start()
-
+            link(packed.at[q, block(way)], got1.at[q, block(way)], s1_send.at[q], s1_recv.at[q], xc_peer(way)).start()
+
+        pack(q)
         last1_got[ways(late * WAYS)] = last1[ways(late * WAYS)]
         got1[q, 0:BLOCK, :] = packed[q, 0:BLOCK, :]
         each(1, WAYS, code)
@@ -219,30 +215,28 @@
     def leave_early(q):
         def code(way):
             at = q * WAYS + way
-            link(code1.at[at], code1_got.at[at], c1_send.at[at], c1_recv.at[at], yz_peer(q, way)).start()
+            link(code1.at[at], code1_got.at[at], c1_send.at[q], c1_recv.at[q], yz_peer(q, way)).start()
 
         def rows(way):
-            at = q * WAYS + way
-            link(packed.at[q, block(way)], got1.at[q, block(way)], s1_send.at[at], s1_recv.at[at], yz_peer(q, way)).start()
+            link(packed.at[q, block(way)], got1.at[q, block(way)], s1_send.at[q], s1_recv.at[q], yz_peer(q, way)).start()
 
         each(start_of(q), WAYS, code)
         each(start_of(q), WAYS, rows)
 
-    def pack_next(n):
-        pack(lax.rem(n + SPLIT, CHUNKS))
-
     def signal(dy):
         pl.semaphore_signal(gate, 1, device_id=yz_peer(dy, 0), device_id_type=MESH)
 
-    each(0, LATE + 1, pack_next)
-    pl.semaphore_wait(barrier, greeted)
+    pack(0)
     code1_got[0] = code1[0]
     got1[0, 0:BLOCK, :] = packed[0, 0:BLOCK, :]
-    leave_late(SPLIT)
+    pl.semaphore_wait(barrier, greeted)
     leave_early(0)
     each(1, NY, signal)
-    each(SPLIT + 1, CHUNKS, leave_late)
-    each(LATE + 1, CHUNKS, pack_next)
+    codes = code_rows(iota((LATE * PAIRS, ROWS), 0) + SPLIT * PAIRS == bin_of, hop1 * SLOTS + rank)
+    for r in range(LATE * PAIRS):
+        last1[r] = codes[r : r + 1, :]
+    each(SPLIT, CHUNKS, leave_late)
+    each(1, SPLIT, pack)
     pl.semaphore_wait(gate, NY - 1)
     each(1, SPLIT, leave_early)
 
@@ -267,28 +261,18 @@
     def pass_late(q):
         late = q - SPLIT
 
-        def codes(way):
-            at = late * WAYS + way
-            arrived(last1_got.at[ways(at)], c1_send.at[EARLY + at], c1_recv.at[EARLY + at])
-
-        def rows(way):
-            at = q * WAYS + way
-            arrived(got1.at[q, block(way)], s1_send.at[at], s1_recv.at[at])
-
         def codes_on(way):
             at = late * WAYS + way
-            device = yz_peer(q, near_z(way))
-            link(last_mid.at[at], last2.at[at], c2_send.at[EARLY + at], c2_recv.at[EARLY + at], device).start()
+            link(last_mid.at[at], last2.at[at], c2_send.at[q], c2_recv.at[q], yz_peer(q, near_z(way))).start()
 
         def rows_on(way):
-            at = q * WAYS + way
-            device = yz_peer(q, near_z(way))
-            link(mid.at[q, block(way)], got2.at[q, block(way)], s2_send.at[at], s2_recv.at[at], device).start()
-
-        each(1, WAYS, codes)
+            half = s2_recv.at[SPLIT + late * 2 + lax.div(way, WAYS // 2)]
+            link(mid.at[q, block(way)], got2.at[q, block(way)], s2_send.at[q], half, yz_peer(q, near_z(way))).start()
+
+        arrived(last1_got.at[pl.ds(late * PAIRS + WAYS, PAIRS - WAYS)], c1_send.at[q], c1_recv.at[q])
         last_mid[ways(late)] = sum(last1_got[pl.ds(late * PAIRS + way * WAYS, WAYS)] for way in range(WAYS))
         each(0, WAYS, codes_on)
-        each(1, WAYS, rows)
+        arrived(got1.at[q, pl.ds(BLOCK, CHUNK_ROWS - BLOCK)], s1_send.at[q], s1_recv.at[q])
         regroup(q)
         each(0, WAYS, rows_on)
 
@@ -303,11 +287,21 @@
 
     each(0, MESO_DEV * KF // 32, norms)
 
-    def clear(i):
-        rows = pl.ds(pl.multiple_of(i * 32, 32), 32)
-        sums[rows, :] = jnp.zeros((32, D), F32)
-
-    each(0, MESO_DEV * FGROUP // 32, clear)
+    load_old.wait()
+
+    def begin(m):
+        rows = pl.ds(pl.multiple_of(m * FGROUP, FGROUP), FGROUP)
+        mine = pl.ds(pl.multiple_of(m * KF + x * FGROUP, FGROUP), FGROUP)
+        sums[rows, :] = cent[mine, :].astype(F32) - old[pl.ds(m, 1), :]
+
+    each(0, MESO_DEV, begin)
+    from_row = jnp.where(is_last, bin_of - SPLIT * PAIRS + EARLY, first)
+
+    def from_rows(i):
+        rows = pl.ds(pl.multiple_of(i * 16, 16), 16)
+        row_hot[rows, :] = (iota((16, ROWS), 0) + i * 16 == from_row).astype(F32).astype(BF16)
+
+    each(0, (EARLY + LATE * PAIRS) // 16, from_rows)
     counts[...] = jnp.zeros_like(counts)
     msum[...] = jnp.zeros_like(msum)
     mcount[...] = jnp.zeros_like(mcount)
@@ -362,71 +356,68 @@
     def spread_of(near, hit, pick):
         return sum(dot(piece, pick, NT) for piece in split3(jnp.where(hit, near, 0.0)))
 
+    def early_rows(step, q, ref, send_sem, recv_sem):
+        @pl.when(q == 0)
+        def _():
+            step(ref(1), send_sem, recv_sem)
+
+        @pl.when(q > 0)
+        def _():
+            step(ref(0), send_sem, recv_sem)
+
+    def tail_of(ref, q):
+        return lambda way: ref.at[pl.ds(q * WAYS + way, WAYS - way)]
+
+    def rows_of(ref, q):
+        return lambda way: ref.at[q, pl.ds(way * BLOCK, CHUNK_ROWS - way * BLOCK)]
+
+    def tiles_of(ref, q):
+        return ref.at[pl.ds(q * PAIRS + WAYS, PAIRS - WAYS)]
+
     def pass_on(q):
-        def codes(way):
-            at = q * WAYS + way
-            arrived(code1_got.at[at], c1_send.at[at], c1_recv.at[at])
-
-        def rows(way):
-            at = q * WAYS + way
-            arrived(got1.at[q, block(way)], s1_send.at[at], s1_recv.at[at])
-
         def codes_on(way):
             at = q * WAYS + way
-            link(code1_got.at[ways(q)], code2.at[ways(at)], c2_send.at[at], c2_recv.at[at], xc_peer(way)).start()
+            link(code1_got.at[ways(q)], code2.at[ways(at)], c2_send.at[q], c2_recv.at[q], xc_peer(way)).start()
 
         def rows_on(way):
-            at = q * WAYS + way
-            link(mid.at[q, block(way)], got2.at[q, block(way)], s2_send.at[at], s2_recv.at[at], xc_peer(way)).start()
-
-        each(start_of(q), WAYS, codes)
+            link(mid.at[q, block(way)], got2.at[q, block(way)], s2_send.at[q], s2_recv.at[q], xc_peer(way)).start()
+
+        early_rows(arrived, q, tail_of(code1_got, q), c1_send.at[q], c1_recv.at[q])
         code2[ways(q * WAYS)] = code1_got[ways(q)]
         each(1, WAYS, codes_on)
-        each(start_of(q), WAYS, rows)
+        early_rows(arrived, q, rows_of(got1, q), s1_send.at[q], s1_recv.at[q])
         regroup(q)
         got2[q, 0:BLOCK, :] = mid[q, 0:BLOCK, :]
         each(1, WAYS, rows_on)
 
     def work(q):
-        def codes(way):
-            at = q * WAYS + way
-            arrived(code2.at[ways(at)], c2_send.at[at], c2_recv.at[at])
-
-        def rows(way):
-            at = q * WAYS + way
-            arrived(got2.at[q, block(way)], s2_send.at[at], s2_recv.at[at])
-
         row = iota((LANES, CHUNK_ROWS), 1)
         pick = (iota((LANES, CHUNK_ROWS), 0) == div48(row) * SLOTS + row - 6 * div6(row)).astype(F32).astype(BF16)
         hit = iota((WAYS * WAYS, CHUNK_ROWS), 0) == div6(iota((WAYS * WAYS, CHUNK_ROWS), 1))
-        each(1, WAYS, codes)
-        tile = code2[pl.ds(q * WAYS * WAYS, WAYS * WAYS)].reshape(WAYS * WAYS, LANES)
+        arrived(tiles_of(code2, q), c2_send.at[q], c2_recv.at[q])
+        tile = code2[pl.ds(q * PAIRS, PAIRS)].reshape(PAIRS, LANES)
         high, low = codes_from(tile, hit, pick)
-        each(1, WAYS, rows)
+        arrived(got2.at[q, pl.ds(BLOCK, CHUNK_ROWS - BLOCK)], s2_send.at[q], s2_recv.at[q])
         members = got2[q]
         spread = spread_of(nearest(members, high), hit, pick)
-        for r in range(WAYS * WAYS):
-            ret1[q * WAYS * WAYS + r] = spread[r : r + 1, :]
+        for r in range(PAIRS):
+            ret1[q * PAIRS + r] = spread[r : r + 1, :]
         ret1_got[ways(q * WAYS)] = ret1[ways(q * WAYS)]
 
         def back(way):
-            at = q * WAYS + way
-            link(ret1.at[ways(at)], ret1_got.at[ways(at)], r1_send.at[at], r1_recv.at[at], xc_back(way)).start()
+            at = ways(q * WAYS + way)
+            link(ret1.at[at], ret1_got.at[at], r1_send.at[q], r1_recv.at[q], xc_back(way)).start()
 
         each(1, WAYS, back)
         add_meso(members, high)
         add_fine(members, high, low)
 
     def pass_back(q):
-        def wait(way):
-            at = q * WAYS + way
-            arrived(ret1_got.at[ways(at)], r1_send.at[at], r1_recv.at[at])
-
         def back(way):
             at = q * WAYS + way
-            link(ret_mid.at[at], ret2.at[at], r2_send.at[at], r2_recv.at[at], yz_back(q, way)).start()
-
-        each(1, WAYS, wait)
+            link(ret_mid.at[at], ret2.at[at], r2_send.at[q], r2_recv.at[q], yz_back(q, way)).start()
+
+        arrived(tiles_of(ret1_got, q), r1_send.at[q], r1_recv.at[q])
         ret_mid[ways(q)] = sum(ret1_got[pl.ds((q * WAYS + way) * WAYS, WAYS)] for way in range(WAYS))
         each(start_of(q), WAYS, back)
 
@@ -440,10 +431,17 @@
         work(i)
 
     each(0, SPLIT, turn)
-    load_old.wait()
-
-    def late_codes(at):
-        arrived(last2.at[at], c2_send.at[EARLY + at], c2_recv.at[EARLY + at])
+
+    def early_left(q):
+        early_rows(left, q, rows_of(packed, q), s1_send.at[q], s1_recv.at[q])
+        early_rows(left, q, tail_of(code1, q), c1_send.at[q], c1_recv.at[q])
+        left(mid.at[q, pl.ds(BLOCK, CHUNK_ROWS - BLOCK)], s2_send.at[q], s2_recv.at[q])
+        left(tiles_of(code2, q), c2_send.at[q], c2_recv.at[q])
+        left(tiles_of(ret1, q), r1_send.at[q], r1_recv.at[q])
+
+    def late_left(q):
+        left(packed.at[q, pl.ds(BLOCK, CHUNK_ROWS - BLOCK)], s1_send.at[q], s1_recv.at[q])
+        left(tiles_of(last1, q - SPLIT), c1_send.at[q], c1_recv.at[q])
 
     def late_half(n):
         q = SPLIT + lax.div(n, 2)
@@ -455,17 +453,13 @@
 
         @pl.when(h == 0)
         def _():
-            each(late * WAYS, late * WAYS + WAYS, late_codes)
+            arrived(last2.at[ways(late)], c2_send.at[q], c2_recv.at[q])
 
         high, low = codes_from(last2[ways(late)].reshape(WAYS, LANES), hit, pick)
 
-        def rows(way):
-            at = q * WAYS + way
-            arrived(got2.at[q, block(way)], s2_send.at[at], s2_recv.at[at])
-
-        start = h * (WAYS // 2)
-        each(start, start + WAYS // 2, rows)
-        members = got2[q, pl.ds(pl.multiple_of(h * HALF, HALF), HALF), :]
+        half = pl.ds(pl.multiple_of(h * HALF, HALF), HALF)
+        arrived(got2.at[q, half], s2_send.at[q], s2_recv.at[SPLIT + n])
+        members = got2[q, half, :]
         add_meso(members, high)
 
         @pl.when(n == 2 * LATE - 1)
@@ -476,7 +470,7 @@
             def share_out(dx):
                 share = pl.ds(pl.multiple_of(lax.rem(x + dx, NX) * SHARE, SHARE), SHARE)
                 device = xc_peer(dx * NC)
-                link(part.at[share], part_got.at[dx - 1], p_send.at[dx - 1], p_recv.at[dx - 1], device).start()
+                link(part.at[share], part_got.at[dx - 1], p_send, p_recv, device).start()
 
             each(1, NX, share_out)
 
@@ -486,128 +480,77 @@
             def _():
                 back1[late * WAYS + r] = spread[r : r + 1, :]
 
-        def back(way):
-            at = late * WAYS + way
-            device = yz_back(q, near_z(way))
-            link(back1.at[at], back1_got.at[at], r1_send.at[EARLY + at], r1_recv.at[EARLY + at], device).start()
-
-        each(start, start + WAYS // 2, back)
+        def back(at):
+            way = h * (WAYS // 2) + lax.div(at, WAYS)
+            j = lax.rem(at, WAYS)
+            row = late * WAYS + way
+            to = EARLY + late * PAIRS + j * WAYS + way
+            device = (
+                lax.rem(x + NX - lax.div(j, NC), NX),
+                (lax.rem(y + NY - q, NY) * NZ + lax.rem(z + NZ - near_z(way), NZ)) * NC + lax.rem(c + lax.rem(j, NC), NC),
+            )
+            link(back1.at[row], ret2.at[to], r2_send.at[q], r2_recv.at[q], device).start()
+
+        each(0, PAIRS // 2, back)
         add_fine(members, high, low)
 
         @pl.when(n == 1)
         def _():
             pass_back(SPLIT - 1)
+            each(0, SPLIT, early_left)
+            each(SPLIT, CHUNKS, late_left)
 
     each(0, 2 * LATE, late_half)
     ret2[0] = ret_mid[0]
 
-    def begin(m):
-        rows = pl.ds(pl.multiple_of(m * FGROUP, FGROUP), FGROUP)
-        mine = pl.ds(pl.multiple_of(m * KF + x * FGROUP, FGROUP), FGROUP)
-        sums[rows, :] += cent[mine, :].astype(F32) - old[pl.ds(m, 1), :]
-
-    each(0, MESO_DEV, begin)
-
-    each(1, NX, lambda dx: arrived(part_got.at[dx - 1], p_send.at[dx - 1], p_recv.at[dx - 1]))
+    inverse[...] = 1.0 / (counts[...] + 1.0)
+
+    arrived(part_got, p_send, p_recv)
     share = pl.ds(pl.multiple_of(x * SHARE, SHARE), SHARE)
     total = (part[share, :] + part_got[1]) + (part_got[0] + part_got[2])
     new_part[...] = (total[:, 0:D] + old[share, :]) / (total[:, D : D + 1] + 1.0)
 
     def hand_out(dx):
-        link(new_part, new_all.at[dx - 1], n_send.at[dx - 1], n_recv.at[dx - 1], xc_peer(dx * NC)).start()
+        link(new_part, new_all.at[dx - 1], n_send, n_recv, xc_peer(dx * NC)).start()
 
     each(1, NX, hand_out)
     new_meso_ref[share, :] = new_part[...]
 
-    def late_back(late):
-        def wait(way):
-            at = late * WAYS + way
-            arrived(back1_got.at[at], r1_send.at[EARLY + at], r1_recv.at[EARLY + at])
-
-        def back(way):
-            at = late * WAYS + way
-            link(
-                back1_got.at[ways(late)], ret2.at[pl.ds(EARLY + at * WAYS, WAYS)], r2_send.at[EARLY + at], r2_recv.at[EARLY + at], xc_back(way)
-            ).start()
-
-        each(0, WAYS, wait)
-        ret2[pl.ds(EARLY + late * PAIRS, WAYS)] = back1_got[ways(late)]
-        each(1, WAYS, back)
-
-    each(0, LATE, late_back)
-
+    arrived(new_all, n_send, n_recv)
     for dx in range(1, NX):
-        arrived(new_all.at[dx - 1], n_send.at[dx - 1], n_recv.at[dx - 1])
         share = pl.ds(pl.multiple_of(lax.rem(x + NX - dx, NX) * SHARE, SHARE), SHARE)
         new_meso_ref[share, :] = new_all[dx - 1]
 
     def finish(m):
         rows = pl.ds(pl.multiple_of(m * FGROUP, FGROUP), FGROUP)
-        new_fine_ref[rows, :] = (sums[rows, :] + new_meso_ref[pl.ds(m, 1), :]) / (counts[rows, :] + 1.0)
+        new_fine_ref[rows, :] = (sums[rows, :] + new_meso_ref[pl.ds(m, 1), :]) * inverse[rows, :]
 
     each(0, MESO_DEV, finish)
 
-    from_row = jnp.where(is_last, bin_of - SPLIT * PAIRS + EARLY, first)
-    row_hot = (iota((EARLY + LATE * PAIRS, ROWS), 0) == from_row).astype(F32).astype(BF16)
     mine = iota((LANES, ROWS), 0) == jnp.where(is_last, hop1, hop2) * SLOTS + rank
-    each(1, EARLY, lambda at: arrived(ret2.at[at], r2_send.at[at], r2_recv.at[at]))
-
-    def late_returned(n):
-        late = lax.div(n, WAYS - 1)
-        at = late * WAYS + 1 + lax.rem(n, WAYS - 1)
-        arrived(ret2.at[pl.ds(EARLY + at * WAYS, WAYS)], r2_send.at[EARLY + at], r2_recv.at[EARLY + at])
-
-    each(0, LATE * (WAYS - 1), late_returned)
+    arrived(ret2.at[pl.ds(1, WAYS - 1)], r2_send.at[0], r2_recv.at[0])
+    for q in range(1, SPLIT):
+        arrived(ret2.at[ways(q)], r2_send.at[q], r2_recv.at[q])
+    for q in range(SPLIT, CHUNKS):
+        arrived(ret2.at[pl.ds(EARLY + (q - SPLIT) * PAIRS, PAIRS)], r2_send.at[q], r2_recv.at[q])
     returned = ret2[...].reshape(EARLY + LATE * PAIRS, LANES)
-    picked = sum(dot(piece, row_hot, TN) for piece in split3(returned))
+    picked = sum(dot(piece, row_hot[...], TN) for piece in split3(returned))
     near_ref[...] = jnp.sum(jnp.where(mine, picked, 0.0), axis=0, keepdims=True).reshape(ROWS)
 
-    def early_left(at):
-        q = lax.div(at, WAYS)
-        way = lax.rem(at, WAYS)
-        left(packed.at[q, block(way)], s1_send.at[at], s1_recv.at[at])
-        left(code1.at[at], c1_send.at[at], c1_recv.at[at])
-        left(ret_mid.at[at], r2_send.at[at], r2_recv.at[at])
-
-    def early_left2(at):
-        q = lax.div(at, WAYS - 1)
-        way = lax.rem(at, WAYS - 1) + 1
-        at = q * WAYS + way
-        left(mid.at[q, block(way)], s2_send.at[at], s2_recv.at[at])
-        left(code1_got.at[ways(q)], c2_send.at[at], c2_recv.at[at])
-        left(ret1.at[ways(at)], r1_send.at[at], r1_recv.at[at])
-
-    def late_left(n):
-        late = lax.div(n, WAYS - 1)
-        way = lax.rem(n, WAYS - 1) + 1
-        at = EARLY + late * WAYS + way
-        left(packed.at[SPLIT + late, block(way)], s1_send.at[at], s1_recv.at[at])
-        left(last1.at[ways(late * WAYS + way)], c1_send.at[at], c1_recv.at[at])
-        left(back1_got.at[ways(late)], r2_send.at[at], r2_recv.at[at])
-
-    def late_left2(n):
-        late = lax.div(n, WAYS)
-        way = lax.rem(n, WAYS)
-        at = EARLY + n
-        left(mid.at[SPLIT + late, block(way)], s2_send.at[at], s2_recv.at[at])
-        left(last_mid.at[n], c2_send.at[at], c2_recv.at[at])
-        left(back1.at[n], r1_send.at[at], r1_recv.at[at])
-
-    def meso_left(dx):
-        left(part_got.at[dx], p_send.at[dx], p_recv.at[dx])
-        left(new_part, n_send.at[dx], n_recv.at[dx])
-
-    each(1, EARLY, early_left)
-    each(0, SPLIT * (WAYS - 1), early_left2)
-    each(0, LATE * (WAYS - 1), late_left)
-    each(0, LATER, late_left2)
-    each(0, NX - 1, meso_left)
+    left(code1.at[pl.ds(1, WAYS - 1)], r2_send.at[0], r2_recv.at[0])
+    for q in range(1, SPLIT):
+        left(code1.at[ways(q)], r2_send.at[q], r2_recv.at[q])
+    for q in range(SPLIT, CHUNKS):
+        left(mid.at[q], s2_send.at[q], s2_recv.at[q])
+        left(last_mid.at[ways(q - SPLIT)], c2_send.at[q], c2_recv.at[q])
+        left(last1.at[pl.ds((q - SPLIT) * PAIRS, PAIRS)], r2_send.at[q], r2_recv.at[q])
+    left(part_got, p_send, p_recv)
+    left(new_all, n_send, n_recv)
 
 
 def body(vectors, meso_labels, fine_labels, meso_centroids, fine_centroids):
     hbm = pl.BlockSpec(memory_space=pl.ANY)
     vmem = pl.BlockSpec(memory_space=pltpu.VMEM)
-    hops = CHUNKS * WAYS
     dma = pltpu.SemaphoreType.DMA
     outs = (((ROWS,), F32), ((MESO_DEV, D), F32), ((MESO_DEV * FGROUP, D), F32))
 
@@ -634,7 +577,7 @@
             row(EARLY), row(EARLY), row(EARLY * WAYS),
             row(LATE * PAIRS), row(LATE * PAIRS), row(LATER), row(LATER),
             row(EARLY * WAYS), row(EARLY * WAYS), row(EARLY),
-            row(LATER), row(LATER), row(EARLY + LATE * PAIRS),
+            row(LATER), row(EARLY + LATE * PAIRS),
             pltpu.VMEM((MESO_DEV * FGROUP, D), F32),
             pltpu.VMEM((MESO_DEV * FGROUP, 1), F32),
             pltpu.VMEM((MESO_DEV, D), F32),
@@ -648,10 +591,13 @@
             pltpu.VMEM((1, ROWS), I32),
             pltpu.VMEM((1, ROWS), I32),
             pltpu.VMEM((1, ROWS), I32),
+            pltpu.VMEM((EARLY + LATE * PAIRS, ROWS), BF16),
+            pltpu.VMEM((MESO_DEV * FGROUP, 1), F32),
             dma((5,)),
         ]
-        + [dma((hops,)) for _ in range(12)]
-        + [dma((NX - 1,)) for _ in range(4)]
+        + [dma((CHUNKS,)), dma((CHUNKS,)), dma((CHUNKS,)), dma((SPLIT + 2 * LATE,))]
+        + [dma((CHUNKS,)) for _ in range(8)]
+        + [dma] * 4
         + [pltpu.SemaphoreType.REGULAR],
         compiler_params=pltpu.CompilerParams(
             collective_id=0, has_side_effects=True, vmem_limit_bytes=61 * 2**20

time: 110 us -> 103 us (0.936)
  Pallas kernels: 105 us -> 98.7 us
    pallas_call x1, Pallas kernels: 105 us -> 98.7 us  [body(): pl.pallas_call(kernel, out_shape=tuple((pltpu.VMEM(*out) for out in outs)...]
where the time goes in v3:
time: 103 us; the launch traced here: 102 us
  Pallas kernels  98.7 us (96%)
  local copies, waits for them, and re-layouts  2.57 us (2%)
    pallas_call x1, Pallas kernels, body(): pl.pallas_call(kernel, out_shape=tuple((pltpu.VMEM(*out) for out in outs)...  98.7 us
    unnamed x3, local copies, waits for them, and re-layouts  2.57 us

profile of v3, /device:TPU:8, one launch (start us, length us, event | category | flops | bytes accessed | tf_op | source)
XLA Modules:
  0.0 101.9 jit_solution(9193660964147455268)
XLA Ops:
  0.6 98.7 %shard_map.76 = (f32[768]{0:T(1024)S(1)}, f32[32,1024]{1,0:T(8,128)S(1)}, f32[512,1024]{1,0:T(8,128)S(1)}) custom-call(s32[768]{0:T(1024)} %meso_hbm.1, s32[768]{0:T(1024)} %fine_hbm.1, bf16[768,1024]{1,0:T(8,128)(2,1)} %vec_hbm.1, f32[32,1024]{1,0:T(8,128)} %old_hbm.1, bf16[2048,1024]{1,0:T(8,128)(2,1)} %bitcast.3), custom_call_target="tpu_custom_call" | custom-call | tf_op jit(solution)/shard_map/pallas_call | solution.py:560
  99.3 0.6 copy.11
  99.9 0.7 copy.12
  100.6 1.3 %copy.13 = f32[32,16,1024]{2,1,0:T(8,128)} copy(f32[32,16,1024]{2,1,0:T(8,128)S(1)} %bitcast.2) | data formatting | bytes 4194304

commit v4 on v3

--- a/solution.py
+++ b/solution.py
@@ -70,7 +70,7 @@
     meso_ref, fine_ref, vec, old, cent, half_norm, perm, packed, got1, mid, got2,
     code1, code1_got, code2, last1, last1_got, last_mid, last2,
     ret1, ret1_got, ret_mid, back1, ret2,
-    sums, counts, msum, mcount, part, part_got, new_part, new_all,
+    sums, counts, part, part_got, new_part, new_all,
     hot_ref, bin_hot, bin_ref, rank_ref, slot_ref, row_hot, inverse,
     load_sem, s1_send, s1_recv, s2_send, s2_recv, c1_send, c1_recv, c2_send, c2_recv,
     r1_send, r1_recv, r2_send, r2_recv, p_send, p_recv, n_send, n_recv, gate,
@@ -303,8 +303,7 @@
 
     each(0, (EARLY + LATE * PAIRS) // 16, from_rows)
     counts[...] = jnp.zeros_like(counts)
-    msum[...] = jnp.zeros_like(msum)
-    mcount[...] = jnp.zeros_like(mcount)
+    part[...] = jnp.zeros_like(part)
 
     def codes_from(tile, hit, pick):
         tile = tile.astype(I32)
@@ -316,8 +315,8 @@
 
     def add_meso(members, high):
         hot = (iota((MESO_DEV, members.shape[0]), 0) == high).astype(F32)
-        msum[...] += dot(hot.astype(BF16), members)
-        mcount[...] += jnp.sum(hot, axis=1, keepdims=True)
+        part[:, 0:D] += dot(hot.astype(BF16), members)
+        part[:, D : D + LANES] += jnp.broadcast_to(jnp.sum(hot, axis=1, keepdims=True), (MESO_DEV, LANES))
 
     def nearest(members, high):
         size = members.shape[0]
@@ -443,6 +442,9 @@
         left(packed.at[q, pl.ds(BLOCK, CHUNK_ROWS - BLOCK)], s1_send.at[q], s1_recv.at[q])
         left(tiles_of(last1, q - SPLIT), c1_send.at[q], c1_recv.at[q])
 
+    back_x = [lax.rem(x + NX - dx, NX) for dx in range(NX)]
+    back_c = [lax.rem(c + dc, NC) for dc in range(NC)]
+
     def late_half(n):
         q = SPLIT + lax.div(n, 2)
         h = lax.rem(n, 2)
@@ -464,9 +466,6 @@
 
         @pl.when(n == 2 * LATE - 1)
         def _():
-            part[:, 0:D] = msum[...]
-            part[:, D : D + LANES] = jnp.broadcast_to(mcount[...], (MESO_DEV, LANES))
-
             def share_out(dx):
                 share = pl.ds(pl.multiple_of(lax.rem(x + dx, NX) * SHARE, SHARE), SHARE)
                 device = xc_peer(dx * NC)
@@ -474,24 +473,21 @@
 
             each(1, NX, share_out)
 
-        spread = spread_of(nearest(members, high), hit, pick)
-        for r in range(WAYS):
-            @pl.when(h == r // (WAYS // 2))
-            def _():
-                back1[late * WAYS + r] = spread[r : r + 1, :]
-
-        def back(at):
-            way = h * (WAYS // 2) + lax.div(at, WAYS)
-            j = lax.rem(at, WAYS)
+        own_hit = iota((WAYS, HALF), 0) == div48(iota((WAYS, HALF), 1))
+        spread = spread_of(nearest(members, high), own_hit, pick)
+        for r in range(WAYS // 2):
+            back1[late * WAYS + h * (WAYS // 2) + r] = spread[r : r + 1, :]
+
+        def back(i):
+            way = h * (WAYS // 2) + i
             row = late * WAYS + way
-            to = EARLY + late * PAIRS + j * WAYS + way
-            device = (
-                lax.rem(x + NX - lax.div(j, NC), NX),
-                (lax.rem(y + NY - q, NY) * NZ + lax.rem(z + NZ - near_z(way), NZ)) * NC + lax.rem(c + lax.rem(j, NC), NC),
-            )
-            link(back1.at[row], ret2.at[to], r2_send.at[q], r2_recv.at[q], device).start()
-
-        each(0, PAIRS // 2, back)
+            to_row = EARLY + late * PAIRS + way
+            to_yz = (lax.rem(y + NY - q, NY) * NZ + lax.rem(z + NZ - near_z(way), NZ)) * NC
+            for j in range(WAYS):
+                device = (back_x[j // NC], to_yz + back_c[j % NC])
+                link(back1.at[row], ret2.at[to_row + j * WAYS], r2_send.at[q], r2_recv.at[q], device).start()
+
+        each(0, WAYS // 2, back)
         add_fine(members, high, low)
 
         @pl.when(n == 1)
@@ -516,16 +512,13 @@
     each(1, NX, hand_out)
     new_meso_ref[share, :] = new_part[...]
 
-    arrived(new_all, n_send, n_recv)
-    for dx in range(1, NX):
-        share = pl.ds(pl.multiple_of(lax.rem(x + NX - dx, NX) * SHARE, SHARE), SHARE)
-        new_meso_ref[share, :] = new_all[dx - 1]
-
-    def finish(m):
-        rows = pl.ds(pl.multiple_of(m * FGROUP, FGROUP), FGROUP)
-        new_fine_ref[rows, :] = (sums[rows, :] + new_meso_ref[pl.ds(m, 1), :]) * inverse[rows, :]
-
-    each(0, MESO_DEV, finish)
+    def finish(block):
+        first_meso = block * SHARE
+        for m in range(SHARE):
+            rows = pl.ds(pl.multiple_of((first_meso + m) * FGROUP, FGROUP), FGROUP)
+            new_fine_ref[rows, :] = (sums[rows, :] + new_meso_ref[pl.ds(first_meso + m, 1), :]) * inverse[rows, :]
+
+    finish(x)
 
     mine = iota((LANES, ROWS), 0) == jnp.where(is_last, hop1, hop2) * SLOTS + rank
     arrived(ret2.at[pl.ds(1, WAYS - 1)], r2_send.at[0], r2_recv.at[0])
@@ -536,6 +529,15 @@
     returned = ret2[...].reshape(EARLY + LATE * PAIRS, LANES)
     picked = sum(dot(piece, row_hot[...], TN) for piece in split3(returned))
     near_ref[...] = jnp.sum(jnp.where(mine, picked, 0.0), axis=0, keepdims=True).reshape(ROWS)
+
+    arrived(new_all, n_send, n_recv)
+
+    def finish_other(dx):
+        block = lax.rem(x + NX - dx, NX)
+        new_meso_ref[pl.ds(pl.multiple_of(block * SHARE, SHARE), SHARE), :] = new_all[dx - 1]
+        finish(block)
+
+    each(1, NX, finish_other)
 
     left(code1.at[pl.ds(1, WAYS - 1)], r2_send.at[0], r2_recv.at[0])
     for q in range(1, SPLIT):
@@ -580,8 +582,6 @@
             row(LATER), row(EARLY + LATE * PAIRS),
             pltpu.VMEM((MESO_DEV * FGROUP, D), F32),
             pltpu.VMEM((MESO_DEV * FGROUP, 1), F32),
-            pltpu.VMEM((MESO_DEV, D), F32),
-            pltpu.VMEM((MESO_DEV, 1), F32),
             pltpu.VMEM((MESO_DEV, D + LANES), F32),
             pltpu.VMEM((NX - 1, SHARE, D + LANES), F32),
             pltpu.VMEM((SHARE, D), F32),

time: 103 us -> 102 us (level); the launches traced: 102 us -> 102 us
  no operation moved by 1% of the time
where the time goes in v4:
time: 102 us
  Pallas kernels  98.7 us (97%)
  local copies, waits for them, and re-layouts  2.57 us (3%)
    pallas_call x1, Pallas kernels, body(): pl.pallas_call(kernel, out_shape=tuple((pltpu.VMEM(*out) for out in outs)...  98.7 us
    unnamed x3, local copies, waits for them, and re-layouts  2.57 us

profile of v4, /device:TPU:8, one launch (start us, length us, event | category | flops | bytes accessed | tf_op | source)
XLA Modules:
  0.0 101.9 jit_solution(6781109926403553368)
XLA Ops:
  0.6 98.7 %shard_map.76 = (f32[768]{0:T(1024)S(1)}, f32[32,1024]{1,0:T(8,128)S(1)}, f32[512,1024]{1,0:T(8,128)S(1)}) custom-call(s32[768]{0:T(1024)} %meso_hbm.1, s32[768]{0:T(1024)} %fine_hbm.1, bf16[768,1024]{1,0:T(8,128)(2,1)} %vec_hbm.1, f32[32,1024]{1,0:T(8,128)} %old_hbm.1, bf16[2048,1024]{1,0:T(8,128)(2,1)} %bitcast.3), custom_call_target="tpu_custom_call" | custom-call | tf_op jit(solution)/shard_map/pallas_call | solution.py:562
  99.4 0.6 copy.11
  100.0 0.7 copy.12
  100.6 1.3 %copy.13 = f32[32,16,1024]{2,1,0:T(8,128)} copy(f32[32,16,1024]{2,1,0:T(8,128)S(1)} %bitcast.2) | data formatting | bytes 4194304

commit v5 on v4

--- a/solution.py
+++ b/solution.py
@@ -123,9 +123,12 @@
     def greet(device):
         pl.semaphore_signal(barrier, 1, device_id=device, device_id_type=MESH)
 
-    each(1, NZ, lambda dz: greet(yz_peer(0, dz)))
-    each(1, NY, lambda dy: greet(yz_peer(dy, 0)))
-    each(1, WAYS, lambda j: greet(xc_peer(j)))
+    for dz in (4, 3, 5, 2, 6, 1, 7):
+        greet(yz_peer(0, dz))
+    for dy in (2, 1, 3):
+        greet(yz_peer(dy, 0))
+    for j in range(WAYS - 1, 0, -1):
+        greet((lax.rem(x + j // NC, NX), (y * NZ + z) * NC + lax.rem(c + j % NC, NC)))
     greeted = NZ + NY + WAYS - 3
 
     load_meso = pltpu.make_async_copy(meso_hbm, meso_ref, load_sem.at[3])
@@ -213,11 +216,13 @@
         each(1, WAYS, rows)
 
     def leave_early(q):
-        def code(way):
+        def code(i):
+            way = near_z(i)
             at = q * WAYS + way
             link(code1.at[at], code1_got.at[at], c1_send.at[q], c1_recv.at[q], yz_peer(q, way)).start()
 
-        def rows(way):
+        def rows(i):
+            way = near_z(i)
             link(packed.at[q, block(way)], got1.at[q, block(way)], s1_send.at[q], s1_recv.at[q], yz_peer(q, way)).start()
 
         each(start_of(q), WAYS, code)

time: 102 us -> 99.6 us (0.976)
  the two profiles are of different devices: /device:TPU:8 before, /device:TPU:1 now
where the time goes in v5:
time: 99.6 us; the launch traced here: 99.5 us
  Pallas kernels  96.3 us (97%)
  local copies, waits for them, and re-layouts  2.57 us (3%)
    pallas_call x1, Pallas kernels, body(): pl.pallas_call(kernel, out_shape=tuple((pltpu.VMEM(*out) for out in outs)...  96.3 us
    unnamed x3, local copies, waits for them, and re-layouts  2.57 us

profile of v5, /device:TPU:1, one launch (start us, length us, event | category | flops | bytes accessed | tf_op | source)
XLA Modules:
  0.0 99.5 jit_solution(4239389793782049455)
XLA Ops:
  0.6 96.3 %shard_map.76 = (f32[768]{0:T(1024)S(1)}, f32[32,1024]{1,0:T(8,128)S(1)}, f32[512,1024]{1,0:T(8,128)S(1)}) custom-call(s32[768]{0:T(1024)} %meso_hbm.1, s32[768]{0:T(1024)} %fine_hbm.1, bf16[768,1024]{1,0:T(8,128)(2,1)} %vec_hbm.1, f32[32,1024]{1,0:T(8,128)} %old_hbm.1, bf16[2048,1024]{1,0:T(8,128)(2,1)} %bitcast.3), custom_call_target="tpu_custom_call" | custom-call | tf_op jit(solution)/shard_map/pallas_call | solution.py:567
  96.9 0.6 copy.11
  97.5 0.7 copy.12
  98.2 1.3 %copy.13 = f32[32,16,1024]{2,1,0:T(8,128)} copy(f32[32,16,1024]{2,1,0:T(8,128)S(1)} %bitcast.2) | data formatting | bytes 4194304

commit v6 on v5

--- a/solution.py
+++ b/solution.py
@@ -240,10 +240,10 @@
     codes = code_rows(iota((LATE * PAIRS, ROWS), 0) + SPLIT * PAIRS == bin_of, hop1 * SLOTS + rank)
     for r in range(LATE * PAIRS):
         last1[r] = codes[r : r + 1, :]
-    each(SPLIT, CHUNKS, leave_late)
     each(1, SPLIT, pack)
     pl.semaphore_wait(gate, NY - 1)
     each(1, SPLIT, leave_early)
+    each(SPLIT, CHUNKS, leave_late)
 
     def perm_rows(i):
         rows = pl.ds(pl.multiple_of(i * 64, 64), 64)

time: 99.6 us -> 99.4 us (level)
  no operation moved by 1% of the time
where the time goes in v6:
time: 99.4 us; the launch traced here: 99.3 us
  Pallas kernels  96.1 us (97%)
  local copies, waits for them, and re-layouts  2.57 us (3%)
    pallas_call x1, Pallas kernels, body(): pl.pallas_call(kernel, out_shape=tuple((pltpu.VMEM(*out) for out in outs)...  96.1 us
    unnamed x3, local copies, waits for them, and re-layouts  2.57 us

profile of v6, /device:TPU:1, one launch (start us, length us, event | category | flops | bytes accessed | tf_op | source)
XLA Modules:
  0.0 99.3 jit_solution(3416466094668825179)
XLA Ops:
  0.6 96.1 %shard_map.76 = (f32[768]{0:T(1024)S(1)}, f32[32,1024]{1,0:T(8,128)S(1)}, f32[512,1024]{1,0:T(8,128)S(1)}) custom-call(s32[768]{0:T(1024)} %meso_hbm.1, s32[768]{0:T(1024)} %fine_hbm.1, bf16[768,1024]{1,0:T(8,128)(2,1)} %vec_hbm.1, f32[32,1024]{1,0:T(8,128)} %old_hbm.1, bf16[2048,1024]{1,0:T(8,128)(2,1)} %bitcast.3), custom_call_target="tpu_custom_call" | custom-call | tf_op jit(solution)/shard_map/pallas_call | solution.py:567
  96.8 0.6 copy.11
  97.4 0.7 copy.12
  98.0 1.3 %copy.13 = f32[32,16,1024]{2,1,0:T(8,128)} copy(f32[32,16,1024]{2,1,0:T(8,128)S(1)} %bitcast.2) | data formatting | bytes 4194304
